TPU v7x, 512 devices: a whole 4x4x16 slice. The times are simulated.
512 devices in a mesh: rows: 128 (over y, z, core), rep: 4 (over x).
Axes of the slice: x: 4, y: 4, z: 16, core: 2. Of those that a mesh axis runs over, the one named last changes fastest.
Arguments:
- feats: bfloat16 [32768, 128], P('rows'), may hold values from -6 to 6
- edge_w: bfloat16 [32768, 8192], P('rows', 'rep'), may hold values from -0.09375 to 0.09375
- send_rows: int32 [128, 128, 64], P('rows', None, 'rep'), may hold values from 0 to 255
- counts: int32 [128, 128], P('rows'), may hold values from 0 to 64, as said below
- w_one: bfloat16 [128, 256], replicated, may hold values from -0.5 to 0.5
- w_two: bfloat16 [256, 256], replicated, may hold values from -0.375 to 0.375
- cotangent: bfloat16 [32768, 256], P('rows'), may hold values from -0.03125 to 0.03125
Outputs:
- output: bfloat16 [32768, 256], P('rows')
- grad_w1: float32 [128, 256], replicated
- grad_w2: float32 [256, 256], replicated
Inputs may be any that keep to these rules, and one draw needn't show every extreme that they name: `counts`: every receiving block has a source block with all 64 slots live.
All inputs are finite; a program needn't handle non-finite values.
Results may differ from a plain program's by a relative error of at most 0.02.
Values may be sent and summed in bfloat16 or wider, within the bound.
A program may use at most 64 MiB of HBM per device.

v0:
```python
import jax
import jax.numpy as jnp
from jax import lax
from jax.sharding import PartitionSpec as P


def silu_slope(values):
    sigma = jax.nn.sigmoid(values)
    return sigma * (1.0 + values * (1.0 - sigma))


def local(feats, edge_w, send_rows, counts, w_one, w_two, cotangent):
    block_rows = feats.shape[0]
    peer_count = send_rows.shape[1]
    slot_count = send_rows.shape[2]
    member = lax.axis_index("rep")
    slot_ids = member * slot_count + jnp.arange(slot_count, dtype=jnp.int32)
    live_slots = (slot_ids[:, None] < counts[0][None, :]).astype(jnp.bfloat16)
    weights = (edge_w.reshape(block_rows, slot_count, peer_count) * live_slots[None, :, :]).reshape(
        block_rows, slot_count * peer_count
    )
    picked_rows = jnp.transpose(send_rows[0]).reshape(slot_count * peer_count)

    def outgoing(values):
        return jnp.take(values, picked_rows, axis=0).reshape(
            slot_count, peer_count, values.shape[1]
        )

    def combine(incoming):
        return jnp.dot(
            weights,
            incoming.reshape(slot_count * peer_count, incoming.shape[2]),
            preferred_element_type=jnp.float32,
        )

    partial_one = combine(
        lax.all_to_all(outgoing(feats), "rows", split_axis=1, concat_axis=1, tiled=True)
    )
    agg_one = lax.psum(partial_one, "rep").astype(jnp.bfloat16)
    z_one = jnp.dot(agg_one, w_one, preferred_element_type=jnp.float32)
    hidden_part = jax.nn.silu(z_one).astype(jnp.bfloat16)
    partial_two = combine(
        lax.all_to_all(outgoing(hidden_part), "rows", split_axis=1, concat_axis=1, tiled=True)
    )
    agg_two = lax.psum(partial_two, "rep").astype(jnp.bfloat16)
    z_two = jnp.dot(agg_two, w_two, preferred_element_type=jnp.float32)
    output_part = jax.nn.silu(z_two).astype(jnp.bfloat16)
    dz_two = (cotangent.astype(jnp.float32) * silu_slope(z_two)).astype(jnp.bfloat16)
    grad_two = lax.dot_general(
        agg_two, dz_two, (((0,), (0,)), ((), ())), preferred_element_type=jnp.float32
    )
    back_part = lax.dot_general(
        dz_two, w_two, (((1,), (1,)), ((), ())), preferred_element_type=jnp.float32
    ).astype(jnp.bfloat16)
    slot_terms = lax.dot_general(
        weights, back_part, (((0,), (0,)), ((), ())), preferred_element_type=jnp.float32
    )
    returned = lax.all_to_all(
        slot_terms.reshape(slot_count, peer_count, slot_terms.shape[1]).astype(jnp.bfloat16),
        "rows",
        split_axis=1,
        concat_axis=1,
        tiled=True,
    ).astype(jnp.float32)
    row_table = (jnp.arange(block_rows, dtype=jnp.int32)[:, None] == picked_rows[None, :]).astype(
        jnp.float32
    )
    d_partial = jnp.dot(
        row_table,
        returned.reshape(slot_count * peer_count, returned.shape[2]),
        preferred_element_type=jnp.float32,
        precision=lax.Precision.HIGHEST,
    )
    d_hidden = lax.psum(d_partial.astype(jnp.bfloat16), "rep").astype(jnp.float32)
    dz_one = (d_hidden * silu_slope(z_one)).astype(jnp.bfloat16)
    grad_one = lax.dot_general(
        agg_one, dz_one, (((0,), (0,)), ((), ())), preferred_element_type=jnp.float32
    )
    grad_one, grad_two = lax.psum((grad_one, grad_two), "rows")
    return (output_part, grad_one, grad_two)


def solution(mesh):
    in_specs = (
        P("rows", None),
        P("rows", "rep"),
        P("rows", None, "rep"),
        P("rows", None),
        P(),
        P(),
        P("rows", None),
    )
    out_specs = (P("rows", None), P(), P())
    return jax.shard_map(local, mesh=mesh, in_specs=in_specs, out_specs=out_specs, check_vma=False)
```

profile of v0, /device:TPU:1, one launch (start us, length us, event | category | flops | bytes accessed | tf_op | source)
XLA Modules:
  0.0 637.1 jit_solution(9465108621557789141)
XLA Ops:
  7.2 0.0 copy-start
  7.2 0.7 compare_and_fusion
  7.9 0.7 compare_select_fusion
  8.6 0.1 copy.22
  8.8 6.4 %gather_fusion = bf16[2048,128]{1,0:T(8,128)(2,1)S(1)} fusion(bf16[256,128]{1,0:T(8,128)(2,1)} %param.7, s32[2048]{0:T(1024)S(1)} %broadcast_clamp_fusion), kind=kCustom, calls=%fused_computation | custom fusion | bytes 1056768 | tf_op jit(solution)/shard_map/jit(_take)/gather | solution.py:25
  15.2 0.0 copy-start.4
  15.2 0.0 copy-start.1
  15.2 1.2 copy_select_fusion.1
  16.4 20.6 %all-to-all-start = ((bf16[16,128,128]{2,0,1:T(8,128)(2,1)}), bf16[16,128,128]{2,0,1:T(8,128)(2,1)S(1)}, u32[]{:S(2)}, u32[]{:S(2)}) async-start(bf16[16,128,128]{2,0,1:T(8,128)(2,1)} %copy_select_fusion.1), calls=%async_computation | async-start | bytes 1048576 | tf_op jit(solution)/shard_map/all_to_all | solution.py:37
  37.0 0.0 copy-done.4
  37.0 0.1 compare_convert_fusion
  37.1 0.0 copy-start.6
  37.1 33.1 %all-to-all-done = bf16[16,128,128]{2,0,1:T(8,128)(2,1)S(1)} async-done(((bf16[16,128,128]{2,0,1:T(8,128)(2,1)}), bf16[16,128,128]{2,0,1:T(8,128)(2,1)S(1)}, u32[]{:S(2)}, u32[]{:S(2)}) %all-to-all-start) | async-done | bytes 524320 | tf_op jit(solution)/shard_map/all_to_all | solution.py:37
  70.2 0.0 copy-done.1
  70.2 0.4 convolution_bitcast_fusion.1
  70.7 14.6 %all-reduce.9 = bf16[256,128]{1,0:T(8,128)(2,1)S(1)} all-reduce(f32[256,128]{1,0:T(8,128)S(1)} %convolution_bitcast_fusion.1), channel_id=1, replica_groups=mesh['rows'=128,'rep'=4] {'rep'}, use_global_device_ids=true, to_apply=%region_0.1 | all-reduce | flops 32768 | bytes 196608 | tf_op jit(solution)/shard_map/psum | solution.py:39
  85.3 0.0 copy-done.6
  85.3 0.9 multiply_convert_fusion.3
  86.2 7.5 %gather_fusion.1 = bf16[2048,256]{1,0:T(8,128)(2,1)S(1)} fusion(bf16[256,256]{1,0:T(8,128)(2,1)S(1)} %get-tuple-element.5, s32[2048]{0:T(1024)S(1)} %broadcast_clamp_fusion), kind=kCustom, calls=%fused_computation.1 | custom fusion | bytes 2105344 | tf_op jit(solution)/shard_map/jit(_take)/gather | solution.py:25
  93.7 2.1 copy_select_fusion
  95.8 10.9 %all-to-all-start.1 = ((bf16[16,128,256]{2,0,1:T(8,128)(2,1)}), bf16[16,128,256]{2,0,1:T(8,128)(2,1)S(1)}, u32[]{:S(2)}, u32[]{:S(2)}) async-start(bf16[16,128,256]{2,0,1:T(8,128)(2,1)} %copy_select_fusion), calls=%async_computation.1 | async-start | bytes 2097152 | tf_op jit(solution)/shard_map/all_to_all | solution.py:43
  106.7 0.0 all-reduce.6.cloned.1.call-start
  106.8 0.1 lt.59
  106.8 0.1 multiply_bitcast_fusion
  106.9 1.3 copy.31
  108.2 52.8 %all-to-all-done.1 = bf16[16,128,256]{2,0,1:T(8,128)(2,1)S(1)} async-done(((bf16[16,128,256]{2,0,1:T(8,128)(2,1)}), bf16[16,128,256]{2,0,1:T(8,128)(2,1)S(1)}, u32[]{:S(2)}, u32[]{:S(2)}) %all-to-all-start.1) | async-done | bytes 1048608 | tf_op jit(solution)/shard_map/all_to_all | solution.py:43
  161.1 0.8 convolution_bitcast_fusion
  161.9 0.0 copy-start.2
  161.9 0.0 copy-start.5
  161.9 13.7 %all-reduce.10 = bf16[256,256]{1,0:T(8,128)(2,1)S(1)} all-reduce(f32[256,256]{1,0:T(8,128)S(1)} %convolution_bitcast_fusion), channel_id=1, replica_groups=mesh['rows'=128,'rep'=4] {'rep'}, use_global_device_ids=true, to_apply=%region_1.2 | all-reduce | flops 65536 | bytes 393216 | tf_op jit(solution)/shard_map/psum | solution.py:45
  175.6 0.0 copy-done
  175.6 0.9 multiply_convert_fusion.2
  176.5 0.0 copy-done.2
  176.5 0.0 copy-done.5
  176.5 0.7 convolution_convert_fusion
  177.3 0.6 copy.29
  177.9 66.4 %all_to_all.15 = bf16[16,128,256]{2,0,1:T(8,128)(2,1)S(1)} all-to-all(bf16[16,128,256]{2,0,1:T(8,128)(2,1)S(1)} %copy.29), channel_id=1, replica_groups=mesh['rows'=128,'rep'=4] {'rows'}, dimensions={1} | all-to-all | bytes 2097152 | tf_op jit(solution)/shard_map/all_to_all | solution.py:58
  244.3 0.0 copy-start.3
  244.3 0.3 copy.30
  244.6 0.4 copy-done.3
  245.0 1.1 fusion.1
  246.1 0.0 copy-start.7
  246.1 0.0 all-reduce.6.cloned.1.call-update
  246.1 0.0 all-reduce.8.cloned.1.call-start
  246.1 1.0 fusion.9
  247.1 46.0 %all-reduce.6.cloned.1.call-done = bf16[256,256]{1,0:T(8,128)(2,1)} async-done(((bf16[256,256]{1,0:T(8,128)(2,1)}), bf16[256,256]{1,0:T(8,128)(2,1)}) %all-reduce.6.cloned.1.call-update) | async-done | bytes 131088 | tf_op jit(solution)/shard_map/psum | solution.py:74
  293.1 0.0 copy-done.7
  293.1 1.8 fusion.8
  294.9 0.0 all-reduce.8.cloned.1.call-update
  295.0 332.0 %all-reduce.8.cloned.1.call-done = (f32[128,256]{1,0:T(8,128)}, f32[256,256]{1,0:T(8,128)}) async-done(((f32[128,256]{1,0:T(8,128)}, f32[256,256]{1,0:T(8,128)}), (f32[128,256]{1,0:T(8,128)}, f32[256,256]{1,0:T(8,128)})) %all-reduce.8.cloned.1.call-update) | async-done | bytes 393232 | tf_op jit(solution)/shard_map/psum | solution.py:79
  627.0 1.6 copy.49
  628.6 1.7 copy.50
  (3 shorter events, 0.0 us)
Async XLA Ops:
  7.2 168.5 %copy-start = (bf16[256,256]{1,0:T(8,128)(2,1)S(1)}, bf16[256,256]{1,0:T(8,128)(2,1)}, u32[]{:S(2)}) copy-start(bf16[256,256]{1,0:T(8,128)(2,1)} %param.12) | copy-start | bytes 393220
  15.2 21.8 %copy-start.4 = (s32[1,128]{1,0:T(1,128)S(1)}, s32[1,128]{1,0:T(1,128)}, u32[]{:S(2)}) copy-start(s32[1,128]{1,0:T(1,128)} %param.10) | copy-start | bytes 1540
  15.2 55.0 %copy-start.1 = (bf16[256,2048]{1,0:T(8,128)(2,1)S(1)}, bf16[256,2048]{1,0:T(8,128)(2,1)}, u32[]{:S(2)}) copy-start(bf16[256,2048]{1,0:T(8,128)(2,1)} %param.8) | copy-start | bytes 3145732
  16.4 53.8 %all-to-all-start = ((bf16[16,128,128]{2,0,1:T(8,128)(2,1)}), bf16[16,128,128]{2,0,1:T(8,128)(2,1)S(1)}, u32[]{:S(2)}, u32[]{:S(2)}) async-start(bf16[16,128,128]{2,0,1:T(8,128)(2,1)} %copy_select_fusion.1), calls=%async_computation | async-start | bytes 1048576 | tf_op jit(solution)/shard_map/all_to_all | solution.py:37
  37.1 48.2 %copy-start.6 = (bf16[128,256]{1,0:T(8,128)(2,1)S(1)}, bf16[128,256]{1,0:T(8,128)(2,1)}, u32[]{:S(2)}) copy-start(bf16[128,256]{1,0:T(8,128)(2,1)} %param.11) | copy-start | bytes 196612
  95.8 65.3 %all-to-all-start.1 = ((bf16[16,128,256]{2,0,1:T(8,128)(2,1)}), bf16[16,128,256]{2,0,1:T(8,128)(2,1)S(1)}, u32[]{:S(2)}, u32[]{:S(2)}) async-start(bf16[16,128,256]{2,0,1:T(8,128)(2,1)} %copy_select_fusion), calls=%async_computation.1 | async-start | bytes 2097152 | tf_op jit(solution)/shard_map/all_to_all | solution.py:43
  106.7 186.4 %all-reduce.6.cloned.1.call-start = ((), (), s32[]{:S(2)}) async-start(), calls=%async_computation.3 | async-start | bytes 262144 | tf_op jit(solution)/shard_map/psum | solution.py:74
  161.9 14.7 %copy-start.2 = (bf16[2048,256]{1,0:T(8,128)(2,1)S(1)}, bf16[2048,256]{1,0:T(8,128)(2,1)}, u32[]{:S(2)}) copy-start(bf16[2048,256]{1,0:T(8,128)(2,1)} %copy.31) | copy-start | bytes 3145732
  161.9 14.7 %copy-start.5 = (bf16[256,256]{1,0:T(8,128)(2,1)S(1)}, bf16[256,256]{1,0:T(8,128)(2,1)}, u32[]{:S(2)}) copy-start(bf16[256,256]{1,0:T(8,128)(2,1)} %param.13) | copy-start | bytes 393220
  244.3 0.7 copy-start.3
  246.1 47.1 %copy-start.7 = (f32[256,256]{1,0:T(8,128)S(1)}, f32[256,256]{1,0:T(8,128)}, u32[]{:S(2)}) copy-start(f32[256,256]{1,0:T(8,128)} %get-tuple-element.6) | copy-start | bytes 786436
  246.1 380.9 %all-reduce.8.cloned.1.call-start = ((), (), s32[]{:S(2)}) async-start(), calls=%async_computation.4 | async-start | bytes 786432 | tf_op jit(solution)/shard_map/psum | solution.py:79
Sparse Core Ops, SparseCore 0:
  246.2 46.8 all-reduce.5
  297.6 329.3 all-reduce.7
where the time goes:
time: 638 us; the launch traced here: 637 us
  waiting for transfers between devices  464 us (73%)
  blocking collectives  94.8 us (15%)
  starting transfers between devices  31.6 us (5%)
  local copies, waits for them, and re-layouts  20 us (3%)
  between operations  14.2 us (2%)
  matrix products  7.62 us (1%)
    psum x1, waiting for transfers between devices, local(): grad_one, grad_two = lax.psum((grad_one, grad_two), 'rows')  332 us
    all_to_all x1, blocking collectives, local(): lax.all_to_all(slot_terms.reshape(slot_count, peer_count, slot_terms.shap...  66.4 us
    all_to_all x1, waiting for transfers between devices, local(): lax.all_to_all(outgoing(hidden_part), 'rows', split_axis=1, concat_axis=1...  52.8 us
    psum x1, waiting for transfers between devices, local(): lax.psum(d_partial.astype(jnp.bfloat16), 'rep').astype(jnp.float32)  46 us
    all_to_all x1, waiting for transfers between devices, local(): lax.all_to_all(outgoing(feats), 'rows', split_axis=1, concat_axis=1, tile...  33.1 us
    all_to_all x1, starting transfers between devices, local(): lax.all_to_all(outgoing(feats), 'rows', split_axis=1, concat_axis=1, tile...  20.6 us
    psum x1, blocking collectives, local(): agg_one = lax.psum(partial_one, 'rep').astype(jnp.bfloat16)  14.6 us
    gather x2, local copies, waits for them, and re-layouts, outgoing(): jnp.take(values, picked_rows, axis=0)  13.9 us
  transfers between devices with their start and end apart: 4, of which 4 were waited for; matrix products, arithmetic and copies ran while one was open for 0% of the time, Pallas kernels for 0%

commit v1 on v0

v1 whole, which is shorter than its diff:
```python
import functools

import jax
import jax.numpy as jnp
from jax import lax
from jax.experimental import pallas as pl
from jax.experimental.pallas import tpu as pltpu
from jax.sharding import PartitionSpec as P

MESH = pl.DeviceIdType.MESH
BF = jnp.bfloat16
F32 = jnp.float32


def dot(a, b, ca=1, cb=0):
    return lax.dot_general(a, b, (((ca,), (cb,)), ((), ())), preferred_element_type=F32)


def silu_slope(values):
    sigma = jax.nn.sigmoid(values)
    return sigma * (1.0 + values * (1.0 - sigma))


def kernel(
    feats, idxt, cnt, w, w1, w2, cot,
    out, gr1, gr2,
    wtf, wtb, wr, stage, g1, acc1, rb1, sw, g2, acc2, rb2, dd, dt, bk, st0, rsb, ys, yb,
    ga, gb, gy, gz, gt, gq,
    sw_s, sw_r, wx_s, wx_r, y1_s, y1_r, z1_s, z1_r, r1_s, r1_r, sx_s, sx_r, y2_s, y2_r, z2_s, z2_r,
    r2_s, r2_r, ox_s, ox_r, bx_s, bx_r, rs_s, rs_r, ry_s, ry_r,
    ga_s, ga_r, gy_s, gy_r, gz_s, gz_r, gt_s, gt_r, gq_s, gq_r,
):
    r = lax.axis_index("rows")
    x = lax.axis_index("rep")
    core = lax.rem(r, 2)
    z = lax.rem(lax.div(r, 2), 16)
    y = lax.div(r, 32)
    zh = lax.div(z, 8)
    zl = lax.rem(z, 8)
    q = core * 4 + x

    def rid(yy, zz, cc):
        return (yy * 16 + zz) * 2 + cc

    def peer8(m):
        pq = lax.rem(q + m, 8)
        pc, px = lax.div(pq, 4), lax.rem(pq, 4)
        return pq, rid(y, z, pc), px

    def zpeer(m):
        return rid(y, lax.rem(z + m, 16), core)

    def ypeer(m):
        return rid(lax.rem(y + m, 4), z, core)

    def copy(src, dst, ssem, rsem, rows, rep):
        return pltpu.make_async_remote_copy(
            src_ref=src, dst_ref=dst, send_sem=ssem, recv_sem=rsem,
            device_id={"rows": rows, "rep": rep}, device_id_type=MESH,
        )

    alone = jnp.logical_and(x == y, core == zh)
    part_r, part_x = rid(x, core * 8 + zl, zh), y

    barrier = pltpu.get_barrier_semaphore()

    def greet(rows, rep):
        pl.semaphore_signal(barrier, inc=1, device_id={"rows": rows, "rep": rep}, device_id_type=MESH)

    for m in range(1, 8):
        _, pr, px = peer8(m)
        greet(pr, px)
    for m in range(1, 4):
        greet(ypeer(m), x)
    for m in range(1, 16):
        greet(zpeer(m), x)

    @pl.when(jnp.logical_not(alone))
    def _():
        greet(part_r, part_x)

    stage[0:64, :] = feats[pl.ds(pl.multiple_of(x * 64, 64), 64), :]
    stage[64:80, :] = idxt[...].astype(F32).astype(BF)

    pl.semaphore_wait(barrier, 26 - alone.astype(jnp.int32))

    def swap(src, dst, ssem, rsem):
        @pl.when(alone)
        def _():
            dst[...] = src[...]

        c = copy(src, dst, ssem, rsem, part_r, part_x)

        @pl.when(jnp.logical_not(alone))
        def _():
            c.start()

        def finish():
            @pl.when(jnp.logical_not(alone))
            def _():
                c.wait()

        return finish

    swap_done = swap(stage, g1.at[core * 8 + zl, x], sw_s, sw_r)

    for s in range(16):
        t = jnp.where(cnt[...] > x * 16 + s, w[:, s * 128:(s + 1) * 128].astype(F32), 0.0)
        tt = t.T
        for half in range(2):
            wtf[half, pl.ds(s, 128, stride=16), :] = tt[:, half * 128:(half + 1) * 128]
    for half in range(2):
        wtb[:, :, half * 128:(half + 1) * 128] = wtf[half].astype(BF).reshape(128, 16, 128)

    wcopies = []
    for m in range(1, 8):
        pq, pr, px = peer8(m)
        group = px * 2 + lax.div(pq, 4)
        c = copy(wtb.at[pl.ds(group * 16, 16)], wr.at[core, :, x], wx_s.at[m], wx_r.at[m], pr, px)
        c.start()
        wcopies.append(c)
    wr[core, :, x] = wtb[pl.ds((x * 2 + core) * 16, 16)]

    swap_done()

    def gather_y(g, ssem, rsem):
        cs = []
        for m in range(1, 4):
            c = copy(g.at[z, y], g.at[z, y], ssem.at[m], rsem.at[m], ypeer(m), x)
            c.start()
            cs.append(c)
        for c in cs:
            c.wait()

    def zslot(m):
        return lax.rem(z + m + 16, 16)

    def gather_z(g, ssem, rsem, process):
        def hop(d, s, chunk):
            slot = zslot(-s) if d == 0 else zslot(s)
            return copy(g.at[slot, chunk], g.at[slot, chunk], ssem.at[d, s, chunk], rsem.at[d, s, chunk],
                        zpeer(1 if d == 0 else 15), x)

        for chunk in range(4):
            for d in range(2):
                hop(d, 0, chunk).start()
        process(z)

        def body(s, _):
            for chunk in range(4):
                for d in range(2):
                    hop(d, s, chunk).wait_recv()
                    hop(d, s + 1, chunk).start()
            process(zslot(-1 - s))
            process(zslot(1 + s))
            return 0

        lax.fori_loop(0, 6, body, 0)
        for chunk in range(4):
            for d in range(2):
                hop(d, 6, chunk).wait_recv()
                if chunk // 2 == d:
                    hop(d, 7, chunk).start()
        process(zslot(-7))
        process(zslot(7))
        for chunk in range(4):
            hop(chunk // 2, 7, chunk).wait_recv()
        process(zslot(8))

        def sent(s, _):
            for chunk in range(4):
                for d in range(2):
                    hop(d, s, chunk).wait_send()
            return 0

        lax.fori_loop(0, 7, sent, 0)
        for chunk in range(4):
            hop(chunk // 2, 7, chunk).wait_send()

    gather_y(g1, y1_s, y1_r)

    for c in wcopies:
        c.wait()

    i0 = r - core
    lane = lax.broadcasted_iota(jnp.int32, (64, 256), 1).astype(F32)
    row_i = lax.broadcasted_iota(jnp.int32, (128, 256), 0)
    acc1[...] = jnp.zeros_like(acc1)

    def process1(slot):
        c16 = lax.rem(slot, 8) * 2 + lax.div(slot, 8)
        rows = g1[slot, :, 64:80, :].reshape(64, 128)
        vals = g1[slot, :, 0:64, :].reshape(256, 128)
        for g in range(2):
            pick = (row_i == i0 + g).astype(F32).astype(BF)
            oh = (dot(rows, pick) == lane).astype(F32).astype(BF)
            ww = wr[g, c16].reshape(64, 256)
            d = dot(ww, oh, 0, 0).astype(BF)
            dd[slot, g * 256:(g + 1) * 256, :] = d
            dt[slot, :, g * 256:(g + 1) * 256] = dot(oh, ww, 0, 0).astype(BF)
            acc1[g * 256:(g + 1) * 256, :] += dot(d, vals)

    gather_z(g1, z1_s, z1_r, process1)

    def reduce8(acc, rb, ssem, rsem):
        cs = []
        for m in range(1, 8):
            pq, pr, px = peer8(m)
            c = copy(acc.at[pl.ds(pl.multiple_of(pq * 64, 64), 64)], rb.at[m], ssem.at[m], rsem.at[m], pr, px)
            c.start()
            cs.append(c)
        total = acc[pl.ds(pl.multiple_of(q * 64, 64), 64), :]
        for m in range(1, 8):
            cs[m - 1].wait_recv()
            total = total + rb[m]
        for c in cs:
            c.wait_send()
        return total

    sw[0] = reduce8(acc1, rb1, r1_s, r1_r).astype(BF)
    swap(sw.at[0], sw.at[1], sx_s, sx_r)()
    agg1 = sw[1]
    z_one = dot(agg1, w1[...])
    g2[z, y] = (z_one * jax.nn.sigmoid(z_one)).astype(BF)

    acc2[...] = jnp.zeros_like(acc2)

    def process2(slot):
        acc2[...] += dot(dd[slot], g2[slot].reshape(256, 256))

    gather_y(g2, y2_s, y2_r)
    gather_z(g2, z2_s, z2_r, process2)

    agg2 = reduce8(acc2, rb2, r2_s, r2_r).astype(BF)
    z_two = dot(agg2, w2[...])
    mine = pl.ds(pl.multiple_of(x * 64, 64), 64)
    dz2 = (cot[mine, :].astype(F32) * silu_slope(z_two)).astype(BF)
    own = pl.ds(pl.multiple_of(q * 64, 64), 64)
    bk[own, :] = dot(dz2, w2[...], 1, 1).astype(BF)
    bcopies = []
    for m in range(1, 8):
        _, pr, px = peer8(m)
        c = copy(bk.at[own], bk.at[own], bx_s.at[m], bx_r.at[m], pr, px)
        c.start()
        bcopies.append(c)
    out[mine, :] = (z_two * jax.nn.sigmoid(z_two)).astype(BF)
    ocopies = []
    for m in range(1, 4):
        c = copy(out.at[mine], out.at[mine], ox_s.at[m], ox_r.at[m], r, lax.rem(x + m, 4))
        c.start()
        ocopies.append(c)
    grad2 = dot(agg2, dz2, 0, 0)
    ga[:, :, :, 0:256] = grad2.reshape(8, 4, 8, 256)

    rsb[0, 0, 2:4] = jnp.zeros((2, 64, 256), BF)
    rsb[1, 0, 0:2] = jnp.zeros((2, 64, 256), BF)
    for c in bcopies:
        c.wait()

    def terms(slot):
        return dot(dt[slot], bk[...]).reshape(4, 64, 256)

    def hop(d, s, chunk):
        src = st0.at[chunk] if isinstance(s, int) and s == 0 else rsb.at[d, s - 1, chunk]
        return copy(src, rsb.at[d, s, chunk], rs_s.at[d, s, chunk], rs_r.at[d, s, chunk],
                    zpeer(1 if d == 0 else 15), x)

    st0[...] = terms(zslot(8)).astype(BF)
    for chunk in range(4):
        hop(chunk // 2, 0, chunk).start()

    def rs_step(s, first):
        for d in range(2):
            val = terms(zslot(8 - s) if d == 0 else zslot(s - 8))
            for chunk in range(4):
                if not first or chunk // 2 == d:
                    hop(d, s - 1, chunk).wait_recv()
                rsb[d, s - 1, chunk] = (rsb[d, s - 1, chunk].astype(F32) + val[chunk]).astype(BF)
                hop(d, s, chunk).start()

    rs_step(1, True)

    def rs_body(s, _):
        rs_step(s, False)
        return 0

    lax.fori_loop(2, 8, rs_body, 0)
    val = terms(z)
    for chunk in range(4):
        for d in range(2):
            hop(d, 7, chunk).wait_recv()
    ys[...] = val + rsb[0, 7].astype(F32) + rsb[1, 7].astype(F32)
    ycopies = []
    for m in range(1, 4):
        c = copy(ys.at[lax.rem(y + m, 4)], yb.at[m], ry_s.at[m], ry_r.at[m], ypeer(m), x)
        c.start()
        ycopies.append(c)
    dh = ys[y]
    for m in range(1, 4):
        ycopies[m - 1].wait_recv()
        dh = dh + yb[m]
    dz1 = (dh * silu_slope(z_one)).astype(BF)
    grad1 = dot(agg1, dz1, 0, 0).reshape(8, 2, 8, 256)
    for a in range(2):
        for b in range(2):
            ga[:, a * 2 + b, :, 256:384] = grad1[:, a, :, b * 128:(b + 1) * 128]

    cs = []
    for m in range(1, 8):
        pq, pr, px = peer8(m)
        c = copy(ga.at[pq], gb.at[m], ga_s.at[m], ga_r.at[m], pr, px)
        c.start()
        cs.append(c)
    total = ga[q]
    for m in range(1, 8):
        cs[m - 1].wait_recv()
        total = total + gb[m]
    gy[0] = total
    c2 = []
    for m in range(1, 4):
        c = copy(gy.at[0, lax.rem(y + m, 4)], gy.at[m, 0], gy_s.at[m], gy_r.at[m], ypeer(m), x)
        c.start()
        c2.append(c)
    tot = gy[0, y]
    for m in range(1, 4):
        c2[m - 1].wait_recv()
        tot = tot + gy[m, 0]
    gz[0] = tot
    c3 = []
    for m in range(1, 16):
        c = copy(gz.at[0], gz.at[m], gz_s.at[m], gz_r.at[m], zpeer(m), x)
        c.start()
        c3.append(c)
    for c in c3:
        c.wait_recv()
    tot = jnp.zeros((8, 384), F32)
    for k in range(16):
        tot = tot + gz[lax.rem(z - k + 16, 16)]
    gt[y] = tot
    c4 = []
    for m in range(1, 4):
        c = copy(gt.at[y], gt.at[y], gt_s.at[m], gt_r.at[m], ypeer(m), x)
        c.start()
        c4.append(c)
    for c in c4:
        c.wait()
    gq[q] = gt[...]
    c5 = []
    for m in range(1, 8):
        _, pr, px = peer8(m)
        c = copy(gq.at[q], gq.at[q], gq_s.at[m], gq_r.at[m], pr, px)
        c.start()
        c5.append(c)
    for c in c5:
        c.wait()
    gr2[...] = gq[:, :, :, 0:256].reshape(256, 256)
    for a in range(2):
        for b in range(2):
            gr1[:, a, :, b * 128:(b + 1) * 128] = gq[:, a * 2 + b, :, 256:384]

    for c in cs + c2 + c3 + ycopies:
        c.wait_send()
    for c in ocopies:
        c.wait()
    for chunk in range(4):
        hop(chunk // 2, 0, chunk).wait_send()

    def rs_sent(s, _):
        for chunk in range(4):
            for d in range(2):
                hop(d, s, chunk).wait_send()
        return 0

    lax.fori_loop(1, 8, rs_sent, 0)


def local(feats, edge_w, send_rows, counts, w_one, w_two, cotangent):
    idxt = jnp.transpose(send_rows[0])
    vm = pl.BlockSpec(memory_space=pltpu.VMEM)
    dma = pltpu.SemaphoreType.DMA
    scratch = [
        pltpu.VMEM((2, 2048, 128), F32),
        pltpu.VMEM((128, 16, 256), BF),
        pltpu.VMEM((2, 16, 4, 16, 256), BF),
        pltpu.VMEM((80, 128), BF),
        pltpu.VMEM((16, 4, 80, 128), BF),
        pltpu.VMEM((512, 128), F32),
        pltpu.VMEM((8, 64, 128), F32),
        pltpu.VMEM((2, 64, 128), BF),
        pltpu.VMEM((16, 4, 64, 256), BF),
        pltpu.VMEM((512, 256), F32),
        pltpu.VMEM((8, 64, 256), F32),
        pltpu.VMEM((16, 512, 256), BF),
        pltpu.VMEM((16, 256, 512), BF),
        pltpu.VMEM((512, 256), BF),
        pltpu.VMEM((4, 64, 256), BF),
        pltpu.VMEM((2, 8, 4, 64, 256), BF),
        pltpu.VMEM((4, 64, 256), F32),
        pltpu.VMEM((4, 64, 256), F32),
        pltpu.VMEM((8, 4, 8, 384), F32),
        pltpu.VMEM((8, 4, 8, 384), F32),
        pltpu.VMEM((4, 4, 8, 384), F32),
        pltpu.VMEM((16, 8, 384), F32),
        pltpu.VMEM((4, 8, 384), F32),
        pltpu.VMEM((8, 4, 8, 384), F32),
    ]
    one = dma(())
    sems = [
        one, one, dma((8,)), dma((8,)), dma((4,)), dma((4,)), dma((2, 8, 4)), dma((2, 8, 4)),
        dma((8,)), dma((8,)), one, one, dma((4,)), dma((4,)), dma((2, 8, 4)), dma((2, 8, 4)),
        dma((8,)), dma((8,)), dma((4,)), dma((4,)), dma((8,)), dma((8,)),
        dma((2, 8, 4)), dma((2, 8, 4)), dma((4,)), dma((4,)),
        dma((8,)), dma((8,)), dma((4,)), dma((4,)), dma((16,)), dma((16,)), dma((4,)), dma((4,)), dma((8,)), dma((8,)),
    ]
    out, gr1, gr2 = pl.pallas_call(
        kernel,
        out_shape=(
            jax.ShapeDtypeStruct((256, 256), BF),
            jax.ShapeDtypeStruct((8, 2, 8, 256), F32),
            jax.ShapeDtypeStruct((256, 256), F32),
        ),
        in_specs=[vm] * 7,
        out_specs=(vm, vm, vm),
        scratch_shapes=scratch + sems,
        compiler_params=pltpu.CompilerParams(
            collective_id=0, has_side_effects=True, vmem_limit_bytes=48 * 1024 * 1024
        ),
    )(feats, idxt, counts, edge_w, w_one, w_two, cotangent)
    return out, gr1.reshape(128, 256), gr2


def solution(mesh):
    in_specs = (
        P("rows", None),
        P("rows", "rep"),
        P("rows", None, "rep"),
        P("rows", None),
        P(),
        P(),
        P("rows", None),
    )
    out_specs = (P("rows", None), P(), P())
    return jax.shard_map(local, mesh=mesh, in_specs=in_specs, out_specs=out_specs, check_vma=False)
```

time: 638 us -> 199 us (0.31)
  waiting for transfers between devices: 464 us -> 0 us
  Pallas kernels: 0 us -> 190 us
  blocking collectives: 94.8 us -> 0 us
  starting transfers between devices: 31.6 us -> 0 us
  between operations: 14.2 us -> 0.66 us
  local copies, waits for them, and re-layouts: 20 us -> 8.07 us
  matrix products: 7.62 us -> 0 us
    psum x2 -> x0, waiting for transfers between devices: 378 us -> none  [the longest x1 332 us: local(): grad_one, grad_two = lax.psum((grad_one, grad_two), 'rows')]
    pallas_call x0 -> x1, Pallas kernels: none -> 190 us  [local(): pl.pallas_call(kernel, out_shape=(jax.ShapeDtypeStruct((256, 256), BF), j...]
    all_to_all x2 -> x0, waiting for transfers between devices: 85.9 us -> none  [the longest x1 52.8 us: local(): lax.all_to_all(outgoing(hidden_part), 'rows', split_axis=1, concat_axis=1...]
    all_to_all x1 -> x0, blocking collectives: 66.4 us -> none  [local(): lax.all_to_all(slot_terms.reshape(slot_count, peer_count, slot_terms.shap...]
    all_to_all x2 -> x0, starting transfers between devices: 31.5 us -> none  [the longest x1 20.6 us: local(): lax.all_to_all(outgoing(feats), 'rows', split_axis=1, concat_axis=1, tile...]
    psum x2 -> x0, blocking collectives: 28.4 us -> none  [the longest x1 14.6 us: local(): agg_one = lax.psum(partial_one, 'rep').astype(jnp.bfloat16)]
    gather x2 -> x0, local copies, waits for them, and re-layouts: 13.9 us -> none  [outgoing(): jnp.take(values, picked_rows, axis=0)]
    dot_general x8 -> x0, matrix products: 7.62 us -> none  [the longest x1 1.8 us: local(): lax.dot_general(agg_one, dz_one, (((0,), (0,)), ((), ())), preferred_elem...]
  transfers between devices with their start and end apart: 4 -> 0, of which waited for: 4 -> 0; matrix products, arithmetic and copies ran while one was open for 0% -> 0% of each run, Pallas kernels for 0% -> 0%
where the time goes in v1:
time: 199 us; the launch traced here: 198 us
  Pallas kernels  190 us (95%)
  local copies, waits for them, and re-layouts  8.07 us (4%)
    pallas_call x1, Pallas kernels, local(): pl.pallas_call(kernel, out_shape=(jax.ShapeDtypeStruct((256, 256), BF), j...  190 us
    unnamed x17, local copies, waits for them, and re-layouts  8.07 us

profile of v1, /device:TPU:1, one launch (start us, length us, event | category | flops | bytes accessed | tf_op | source)
XLA Modules:
  0.0 198.4 jit_solution(16210183813752332607)
XLA Ops:
  0.6 0.0 copy-start.6
  0.6 0.6 copy-done.6
  1.3 0.0 copy-start
  1.3 1.2 copy-done
  2.5 0.0 copy-start.1
  2.5 0.9 copy-done.1
  3.4 0.0 copy-start.2
  3.4 0.9 copy-done.2
  4.3 0.0 copy-start.3
  4.3 0.8 copy-done.3
  5.2 0.0 copy-start.4
  5.2 0.8 copy-done.4
  6.0 0.0 copy-start.5
  6.0 0.7 copy-done.5
  6.7 189.6 %shard_map.94 = (bf16[256,256]{1,0:T(8,128)(2,1)S(1)}, f32[8,2,8,256]{3,2,1,0:T(8,128)S(1)}, f32[256,256]{1,0:T(8,128)S(1)}) custom-call(bf16[256,128]{1,0:T(8,128)(2,1)S(1)} %copy-done.3, s32[16,128]{1,0:T(8,128)S(1)} %bitcast.5, s32[1,128]{1,0:T(1,128)S(1)} %copy-done.6, bf16[256,2048]{1,0:T(8,128)(2,1)S(1)} %copy-done, bf16[128,256]{1,0:T(8,128)(2,1)S(1)} %copy-done.4, ...), custom_call_target="tpu_custom_call" | custom-call | tf_op jit(solution)/shard_map/pallas_call | solution.py:415
  196.3 0.7 copy.13
  197.0 0.7 copy.14
  197.7 0.7 copy.15
Async XLA Ops:
  0.6 0.7 copy-start.6
  1.3 1.2 copy-start
  2.5 0.9 copy-start.1
  3.4 0.9 copy-start.2
  4.3 0.8 copy-start.3
  5.2 0.8 copy-start.4
  6.0 0.7 copy-start.5

commit v2 on v0

v2 whole, which is shorter than its diff:
```python
import jax
import jax.numpy as jnp
from jax import lax
from jax.experimental import pallas as pl
from jax.experimental.pallas import tpu as pltpu
from jax.sharding import PartitionSpec as P

MESH = pl.DeviceIdType.MESH
BF = jnp.bfloat16
F32 = jnp.float32


def dot(a, b, ca=1, cb=0):
    return lax.dot_general(a, b, (((ca,), (cb,)), ((), ())), preferred_element_type=F32)


def silu_slope(values):
    sigma = jax.nn.sigmoid(values)
    return sigma * (1.0 + values * (1.0 - sigma))


def iota(shape, dim):
    return lax.broadcasted_iota(jnp.int32, shape, dim)


def one_hot(hit):
    return jnp.where(hit, 1.0, 0.0).astype(BF)


def body(
    pending,
    feats_h, idxt_h, cnt_h, w_h, w1_h, w2_h, cot_h,
    out, gr1, gr2,
    feats, idxt, cnt, w, w1, w2, cot,
    wtb, wr, wb, wf, stage, g1, oh, oht, pk, mine1, sum1, rc1, ab1, rp1, sw, g2,
    mine2, sum2, rc2, ab2, rp2, bk, tt, pb, fr, nr, cb,
    in_s, sw_s, sw_r, wx_s, wx_r, z1_s, z1_r, c1_s, c1_r, p1_s, p1_r, sx_s, sx_r, z2_s, z2_r,
    c2_s, c2_r, p2_s, p2_r, ox_s, ox_r, bp_s, bp_r, bc_s, bc_r, fr_s, fr_r, nr_s, nr_r,
    *sums,
):
    r = lax.axis_index("rows")
    x = lax.axis_index("rep")
    core = lax.rem(r, 2)
    z = lax.rem(lax.div(r, 2), 16)
    y = lax.div(r, 32)
    za = lax.div(z, 4)
    zb = lax.rem(z, 4)
    q = y * 4 + x
    other = 1 - core

    def rid(yy, zz, cc):
        return (yy * 16 + zz) * 2 + cc

    def peer(m):
        pq = lax.rem(q + m, 16)
        py, px = lax.div(pq, 4), lax.rem(pq, 4)
        return py, px, rid(py, z, core)

    def zat(m):
        return lax.rem(z + m + 16, 16)

    def zpeer(m):
        return rid(y, zat(m), core)

    def copy(src, dst, ssem, rsem, rows, rep):
        return pltpu.make_async_remote_copy(
            src_ref=src, dst_ref=dst, send_sem=ssem, recv_sem=rsem,
            device_id={"rows": rows, "rep": rep}, device_id_type=MESH,
        )

    def send(src, dst, ssem, rsem, rows, rep):
        c = copy(src, dst, ssem, rsem, rows, rep)
        c.start()
        pending.append(c.wait_send)
        return c

    def to_core(src, dst, ssem, rsem):
        return send(src, dst, ssem, rsem, rid(y, z, other), x)

    barrier = pltpu.get_barrier_semaphore()

    def greet(rows, rep):
        pl.semaphore_signal(barrier, inc=1, device_id={"rows": rows, "rep": rep}, device_id_type=MESH)

    ins = []
    for n, (a, b) in enumerate(
        [(feats_h, feats), (idxt_h, idxt), (cnt_h, cnt), (w_h, w), (w1_h, w1), (w2_h, w2), (cot_h, cot)]
    ):
        c = pltpu.make_async_copy(a, b, in_s.at[n])
        c.start()
        ins.append(c)

    alone = x == zb
    swap_r, swap_x = rid(y, za * 4 + x, core), zb
    for m in range(1, 16):
        greet(zpeer(m), x)
    for m in range(1, 16):
        py, px, pr = peer(m)
        greet(pr, px)
        greet(rid(py, z, other), px)
    greet(rid(y, z, other), x)

    @pl.when(jnp.logical_not(alone))
    def _():
        greet(swap_r, swap_x)

    mine = pl.ds(pl.multiple_of(x * 64, 64), 64)
    ins[0].wait()
    ins[1].wait()
    stage[0:64, :] = feats[mine, :]
    stage[64:80, :] = idxt[...].astype(F32).astype(BF)

    ins[2].wait()
    ins[3].wait()
    row = iota((512, 512), 0)
    plane, rest = row // 16, row % 16
    source = (plane // 8) * 32 + (rest % 4) * 8 + plane % 8
    order = one_hot((rest // 4) * 128 + source == iota((512, 512), 1))
    for sq in range(4):
        parts = []
        for s4 in range(4):
            s = sq * 4 + s4
            parts.append(jnp.where(cnt[...] > x * 16 + s, w[:, s * 128:(s + 1) * 128].astype(F32), 0.0).astype(BF))
        live = jnp.concatenate(parts, axis=1)
        wtb[sq] = dot(order, live, 1, 1).astype(BF).reshape(32, 16, 256)

    pl.semaphore_wait(barrier, 47 - alone.astype(jnp.int32))

    def swap(src, dst, ssem, rsem):
        c = copy(src, dst, ssem, rsem, swap_r, swap_x)

        @pl.when(alone)
        def _():
            dst[...] = src[...]

        @pl.when(jnp.logical_not(alone))
        def _():
            c.start()

        def finish():
            @pl.when(jnp.logical_not(alone))
            def _():
                c.wait_recv()

        def sent():
            @pl.when(jnp.logical_not(alone))
            def _():
                c.wait_send()

        pending.append(sent)
        return finish

    swap_done = swap(stage, g1.at[za * 4 + x], sw_s, sw_r)

    wcopies = []
    me8 = y * 2 + core
    for m in range(1, 16):
        py, px, pr = peer(m)
        for h, hr in ((core, pr), (other, rid(py, z, other))):
            n = 2 * m + (0 if h is core else 1)
            wcopies.append(send(wtb.at[:, (py * 4 + px) * 2 + h], wr.at[me8, x], wx_s.at[n], wx_r.at[n], hr, px))
    wcopies.append(to_core(wtb.at[:, q * 2 + other], wr.at[me8, x], wx_s.at[1], wx_r.at[1]))
    wr[me8, x] = wtb[:, q * 2 + core]
    yield "prep"

    swap_done()
    yield "swap1"

    def gather_z(g, rows, cut, ssem, rsem):
        full, parts = pl.ds(0, rows), (pl.ds(0, cut), pl.ds(cut, rows - cut))

        def move(d, dist):
            sign = 1 if d == 0 else -1
            far = dist > 4
            part = parts[d] if dist == 8 else full
            slot = zat(-sign * 4) if far else z
            return copy(g.at[slot, part], g.at[slot, part], ssem.at[d, dist], rsem.at[d, dist],
                        zpeer(sign * (dist - 4 if far else dist)), x)

        moves = {}
        for dist in (4, 3, 2, 1):
            for d in range(2):
                moves[d, dist] = move(d, dist)
                moves[d, dist].start()
                pending.append(moves[d, dist].wait_send)
        for d in range(2):
            moves[d, 4].wait_recv()
            for dist in (8, 7, 6, 5):
                moves[d, dist] = move(d, dist)
                moves[d, dist].start()
                pending.append(moves[d, dist].wait_send)
        for dist in (1, 2, 3, 5, 6, 7, 8):
            for d in range(2):
                moves[d, dist].wait_recv()

    gather_z(g1, 80, 48, z1_s, z1_r)
    yield "gz1"

    ids = g1[:, 64:80, :].reshape(256, 128)
    lane = iota((256, 256), 1).astype(F32)
    for k in range(8):
        at = ((k // 2) * 16 + z) * 2 + k % 2
        rows = dot(ids, one_hot(iota((128, 256), 0) == at))
        oh[:, k * 64:(k + 1) * 64, :] = one_hot(rows == lane).reshape(4, 64, 256)
    for a in range(4):
        pk[a, :, 0:128] = dot(oh[a], g1[4 * a:4 * a + 4, 0:64, :].reshape(256, 128)).astype(BF)

    yield "picks1"
    for c in wcopies:
        c.wait_recv()
    yield "wwait"

    row, col = iota((256, 256), 0), iota((256, 256), 1)
    regroup = one_hot((row % 64) * 4 + row // 64 == col)
    eye = one_hot(row == col)

    def weights(k):
        wb[k] = dot(regroup, wr[k].reshape(256, 256)).astype(BF)
        wf[k] = dot(eye, wb[k], 1, 1).astype(BF)

    def reduce_planes(width, prepare, own, total, rc, ab, rp, csem_s, csem_r, psem_s, psem_r):
        def partial(k):
            prepare(k)
            picked = pk[:, pl.ds(pl.multiple_of(k * 64, 64), 64), 0:width].reshape(256, width)
            return dot(wf[k], picked)

        cs = []
        for j in range(4):
            own[1, j] = partial(j * 2 + other).astype(BF)
            cs.append(to_core(own.at[1, j], rc.at[j], csem_s.at[j], csem_r.at[j]))
        for j in range(4):
            total[j] = partial(j * 2 + core)
        for j in range(4):
            cs[j].wait_recv()
            ab[j] = (total[j] + rc[j].astype(F32)).astype(BF).reshape(4, 64, width)
        ps = []
        for m in range(1, 16):
            py, px, pr = peer(m)
            ps.append(send(ab.at[py, px], rp.at[m], psem_s.at[m], psem_r.at[m], pr, px))
        res = ab[y, x].astype(F32)
        for m in range(1, 16):
            ps[m - 1].wait_recv()
            res = res + rp[m].astype(F32)
        return res.astype(BF)

    sw[0] = reduce_planes(128, weights, mine1, sum1, rc1, ab1, rp1, c1_s, c1_r, p1_s, p1_r)
    yield "red1"
    swap(sw.at[0], sw.at[1], sx_s, sx_r)()
    yield "swap2"
    for n in (4, 5, 6):
        ins[n].wait()
    agg1 = sw[1]
    z_one = dot(agg1, w1[...])
    g2[z] = (z_one * jax.nn.sigmoid(z_one)).astype(BF)
    gather_z(g2, 64, 32, z2_s, z2_r)
    yield "gz2"
    for a in range(4):
        pk[a] = dot(oh[a], g2[4 * a:4 * a + 4].reshape(256, 256)).astype(BF)
    agg2 = reduce_planes(256, lambda k: None, mine2, sum2, rc2, ab2, rp2, c2_s, c2_r, p2_s, p2_r)
    yield "red2"

    z_two = dot(agg2, w2[...])
    dz2 = (cot[mine, :].astype(F32) * silu_slope(z_two)).astype(BF)
    bk[y, core, mine, :] = dot(dz2, w2[...], 1, 1).astype(BF)
    bcopies = []
    for m in range(1, 16):
        py, px, pr = peer(m)
        bcopies.append(send(bk.at[y, core, mine], bk.at[y, core, mine], bp_s.at[m], bp_r.at[m], pr, px))
    out[mine, :] = (z_two * jax.nn.sigmoid(z_two)).astype(BF)
    ocopies = []
    for m in range(1, 4):
        ocopies.append(send(out.at[mine], out.at[mine], ox_s.at[m], ox_r.at[m], r, lax.rem(x + m, 4)))

    def reduce_all(ga, rc, gs, gp, gz, gt, c_s, c_r, p_s, p_r, z_s, z_r, t_s, t_r, d_s, d_r):
        c = to_core(ga.at[other], rc, c_s, c_r)
        yield
        c.wait_recv()
        gs[...] = ga[core] + rc[...]
        ps = []
        for m in range(1, 16):
            py, px, pr = peer(m)
            ps.append(send(gs.at[py * 4 + px], gp.at[m], p_s.at[m], p_r.at[m], pr, px))
        yield
        total = gs[q]
        for m in range(1, 16):
            ps[m - 1].wait_recv()
            total = total + gp[m]
        gz[0] = total
        zs = []
        for m in (8, 7, 9, 6, 10, 5, 11, 4, 12, 3, 13, 2, 14, 1, 15):
            zs.append(send(gz.at[0], gz.at[m], z_s.at[m], z_r.at[m], zpeer(m), x))
        yield
        for c in zs:
            c.wait_recv()
        total = jnp.zeros_like(total)
        for k in range(16):
            total = total + gz[lax.rem(z - k + 16, 16)]
        gt[core, q] = total
        ts = []
        for m in range(1, 16):
            py, px, pr = peer(m)
            ts.append(send(gt.at[core, q], gt.at[core, q], t_s.at[m], t_r.at[m], pr, px))
        yield
        for c in ts:
            c.wait_recv()
        c = to_core(gt.at[core], gt.at[core], d_s, d_r)
        yield
        c.wait_recv()
        yield

    half = len(sums) // 2
    ga2, ga1 = sums[0], sums[half]
    reduce2, reduce1 = reduce_all(*sums[:half]), reduce_all(*sums[half:])
    ga2[...] = dot(agg2, dz2, 0, 0).reshape(2, 16, 8, 256)
    next(reduce2)

    for a in range(4):
        oht[a] = dot(eye, oh[a], 1, 1).astype(BF)
    for c in bcopies:
        c.wait_recv()
    cc = [to_core(bk.at[j, core], bk.at[j, core], bc_s.at[j], bc_r.at[j]) for j in range(4)]
    next(reduce2)

    def slot_terms(k):
        got = dot(wb[k], bk[lax.div(k, 2), lax.rem(k, 2)]).astype(BF)
        tt[:, pl.ds(pl.multiple_of(k * 64, 64), 64), :] = got.reshape(4, 64, 256)

    for j in range(4):
        slot_terms(j * 2 + core)
    for j in range(4):
        cc[j].wait_recv()
        slot_terms(j * 2 + other)
    yield "bwait"
    for a in range(4):
        pb[4 * a:4 * a + 4] = dot(oht[a], tt[a]).astype(BF).reshape(4, 64, 256)

    full, parts = pl.ds(0, 64), (pl.ds(0, 32), pl.ds(32, 32))
    fars, nears = {}, {}
    for m in (4, 3, 2, 1):
        for d in range(2):
            sign = 1 if d == 0 else -1
            part = parts[d] if m == 4 else full
            fars[d, m] = send(pb.at[zat(sign * (4 + m)), part], fr.at[d, m, part], fr_s.at[d, m], fr_r.at[d, m],
                              zpeer(sign * m), x)
    for m in (3, 2, 1):
        for d in range(2):
            sign = 1 if d == 0 else -1
            nears[d, m] = send(pb.at[zat(sign * m)], nr.at[d, m], nr_s.at[d, m], nr_r.at[d, m], zpeer(sign * m), x)
    next(reduce2)
    for d in range(2):
        sign = 1 if d == 0 else -1
        acc = pb[zat(sign * 4)].astype(F32)
        for m in (1, 2, 3):
            fars[d, m].wait_recv()
            acc = acc + fr[d, m].astype(F32)
        fars[d, 4].wait_recv()
        cb[d] = acc.astype(BF)
        lo = 0 if d == 0 else 32
        cb[d, lo:lo + 32, :] = (acc[lo:lo + 32] + fr[d, 4, lo:lo + 32, :].astype(F32)).astype(BF)
        nears[d, 4] = send(cb.at[d], nr.at[d, 4], nr_s.at[d, 4], nr_r.at[d, 4], zpeer(sign * 4), x)
    next(reduce2)
    dh = pb[z].astype(F32)
    for m in (1, 2, 3, 4):
        for d in range(2):
            nears[d, m].wait_recv()
            dh = dh + nr[d, m].astype(F32)
    yield "rsz"
    dz1 = (dh * silu_slope(z_one)).astype(BF)
    grad1 = dot(agg1, dz1, 0, 0).reshape(2, 8, 8, 256)
    for b in range(2):
        ga1[:, :, b] = grad1[:, :, :, b * 128:(b + 1) * 128]
    ga1 = ga1.reshape(2, 16, 8, 128)
    reduce1 = reduce_all(ga1, *sums[half + 1:])
    next(reduce1)
    next(reduce2)
    yield "arc"
    next(reduce1)
    next(reduce2)
    gr2[...] = sums[5][...].reshape(256, 256)
    yield "arp"
    next(reduce1)
    yield "arz"
    next(reduce1)
    yield "art"
    next(reduce1)
    next(reduce1)
    gt1 = sums[half + 5]
    for b in range(2):
        for k in range(8):
            gr1[:, k, :, b * 128:(b + 1) * 128] = gt1[:, 2 * k + b]
    for c in ocopies:
        c.wait_recv()


def kernel(*refs):
    pending = []
    for _ in body(pending, *refs):
        pass
    for wait in pending:
        wait()


def local(feats, edge_w, send_rows, counts, w_one, w_two, cotangent):
    idxt = jnp.transpose(send_rows[0])
    vm = pl.BlockSpec(memory_space=pltpu.VMEM)
    hbm = pl.BlockSpec(memory_space=pl.ANY)
    args = (feats, idxt, counts, edge_w, w_one, w_two, cotangent)
    dma = pltpu.SemaphoreType.DMA

    def vmem(kind, *shape):
        return pltpu.VMEM(shape, kind)

    scratch = [pltpu.VMEM(a.shape, a.dtype) for a in args] + [
        vmem(BF, 4, 32, 16, 256),
        vmem(BF, 8, 4, 4, 16, 256),
        vmem(BF, 8, 256, 256),
        vmem(BF, 8, 256, 256),
        vmem(BF, 80, 128),
        vmem(BF, 16, 80, 128),
        vmem(BF, 4, 512, 256),
        vmem(BF, 4, 256, 512),
        vmem(BF, 4, 512, 256),
        vmem(BF, 2, 4, 256, 128),
        vmem(F32, 4, 256, 128),
        vmem(BF, 4, 256, 128),
        vmem(BF, 4, 4, 64, 128),
        vmem(BF, 16, 64, 128),
        vmem(BF, 2, 64, 128),
        vmem(BF, 16, 64, 256),
        vmem(BF, 2, 4, 256, 256),
        vmem(F32, 4, 256, 256),
        vmem(BF, 4, 256, 256),
        vmem(BF, 4, 4, 64, 256),
        vmem(BF, 16, 64, 256),
        vmem(BF, 4, 2, 256, 256),
        vmem(BF, 4, 512, 256),
        vmem(BF, 16, 64, 256),
        vmem(BF, 2, 5, 64, 256),
        vmem(BF, 2, 5, 64, 256),
        vmem(BF, 2, 64, 256),
        dma((7,)), dma(()), dma(()), dma((32,)), dma((32,)), dma((2, 9)), dma((2, 9)),
        dma((4,)), dma((4,)), dma((16,)), dma((16,)), dma(()), dma(()), dma((2, 9)), dma((2, 9)),
        dma((4,)), dma((4,)), dma((16,)), dma((16,)), dma((4,)), dma((4,)), dma((16,)), dma((16,)),
        dma((4,)), dma((4,)), dma((2, 5)), dma((2, 5)), dma((2, 5)), dma((2, 5)),
    ]
    for width, first in ((256, (2, 16, 8, 256)), (128, (2, 8, 2, 8, 128))):
        scratch += [
            vmem(F32, *first),
            vmem(F32, 16, 8, width),
            vmem(F32, 16, 8, width),
            vmem(F32, 16, 8, width),
            vmem(F32, 16, 8, width),
            vmem(F32, 2, 16, 8, width),
            dma(()), dma(()), dma((16,)), dma((16,)), dma((16,)), dma((16,)), dma((16,)), dma((16,)), dma(()), dma(()),
        ]
    out, gr1, gr2 = pl.pallas_call(
        kernel,
        out_shape=(
            jax.ShapeDtypeStruct((256, 256), BF),
            jax.ShapeDtypeStruct((2, 8, 8, 256), F32),
            jax.ShapeDtypeStruct((256, 256), F32),
        ),
        in_specs=[hbm] * 7,
        out_specs=(vm, vm, vm),
        scratch_shapes=scratch,
        compiler_params=pltpu.CompilerParams(
            collective_id=0, has_side_effects=True, vmem_limit_bytes=56 * 1024 * 1024
        ),
    )(*args)
    return out, gr1.reshape(128, 256), gr2


def solution(mesh):
    in_specs = (
        P("rows", None),
        P("rows", "rep"),
        P("rows", None, "rep"),
        P("rows", None),
        P(),
        P(),
        P("rows", None),
    )
    out_specs = (P("rows", None), P(), P())
    return jax.shard_map(local, mesh=mesh, in_specs=in_specs, out_specs=out_specs, check_vma=False)
```

time: 638 us -> 135 us (0.21)
  waiting for transfers between devices: 464 us -> 0 us
  Pallas kernels: 0 us -> 132 us
  blocking collectives: 94.8 us -> 0 us
  starting transfers between devices: 31.6 us -> 0 us
  local copies, waits for them, and re-layouts: 20 us -> 2.98 us
  between operations: 14.2 us -> 0.66 us
  matrix products: 7.62 us -> 0 us
    psum x2 -> x0, waiting for transfers between devices: 378 us -> none  [the longest x1 332 us: local(): grad_one, grad_two = lax.psum((grad_one, grad_two), 'rows')]
    pallas_call x0 -> x1, Pallas kernels: none -> 132 us  [local(): pl.pallas_call(kernel, out_shape=(jax.ShapeDtypeStruct((256, 256), BF), j...]
    all_to_all x2 -> x0, waiting for transfers between devices: 85.9 us -> none  [the longest x1 52.8 us: local(): lax.all_to_all(outgoing(hidden_part), 'rows', split_axis=1, concat_axis=1...]
    all_to_all x1 -> x0, blocking collectives: 66.4 us -> none  [local(): lax.all_to_all(slot_terms.reshape(slot_count, peer_count, slot_terms.shap...]
    all_to_all x2 -> x0, starting transfers between devices: 31.5 us -> none  [the longest x1 20.6 us: local(): lax.all_to_all(outgoing(feats), 'rows', split_axis=1, concat_axis=1, tile...]
    psum x2 -> x0, blocking collectives: 28.4 us -> none  [the longest x1 14.6 us: local(): agg_one = lax.psum(partial_one, 'rep').astype(jnp.bfloat16)]
    gather x2 -> x0, local copies, waits for them, and re-layouts: 13.9 us -> none  [outgoing(): jnp.take(values, picked_rows, axis=0)]
    dot_general x8 -> x0, matrix products: 7.62 us -> none  [the longest x1 1.8 us: local(): lax.dot_general(agg_one, dz_one, (((0,), (0,)), ((), ())), preferred_elem...]
  transfers between devices with their start and end apart: 4 -> 0, of which waited for: 4 -> 0; matrix products, arithmetic and copies ran while one was open for 0% -> 0% of each run, Pallas kernels for 0% -> 0%
where the time goes in v2:
time: 135 us
  Pallas kernels  132 us (98%)
  local copies, waits for them, and re-layouts  2.98 us (2%)
    pallas_call x1, Pallas kernels, local(): pl.pallas_call(kernel, out_shape=(jax.ShapeDtypeStruct((256, 256), BF), j...  132 us
    unnamed x7, local copies, waits for them, and re-layouts  2.98 us

profile of v2, /device:TPU:1, one launch (start us, length us, event | category | flops | bytes accessed | tf_op | source)
XLA Modules:
  0.0 135.2 jit_solution(7053479173879653179)
XLA Ops:
  0.6 131.5 %shard_map.94 = (bf16[256,256]{1,0:T(8,128)(2,1)}, f32[2,8,8,256]{3,2,1,0:T(8,128)}, f32[256,256]{1,0:T(8,128)}) custom-call(bf16[256,128]{1,0:T(8,128)(2,1)} %refs_0_.1, s32[16,128]{1,0:T(8,128)} %bitcast.5, s32[1,128]{1,0:T(1,128)} %refs_2_.1, bf16[256,2048]{1,0:T(8,128)(2,1)} %refs_3_.1, bf16[128,256]{1,0:T(8,128)(2,1)} %refs_4_.1, ...), custom_call_target="tpu_custom_call" | custom-call | tf_op jit(solution)/shard_map/pallas_call | solution.py:456
  132.2 0.0 copy-start.1
  132.2 0.0 copy-start
  132.2 1.6 %copy.13 = bf16[256,256]{1,0:T(8,128)(2,1)} copy(bf16[256,256]{1,0:T(8,128)(2,1)} %get-tuple-element.12) | data formatting | bytes 262144
  133.8 0.0 copy-done.1
  133.8 0.7 copy.14
  134.5 0.0 copy-done
  134.5 0.7 copy.15
Async XLA Ops:
  132.2 1.6 %copy-start.1 = (f32[2,8,8,256]{3,2,1,0:T(8,128)S(1)}, f32[2,8,8,256]{3,2,1,0:T(8,128)}, u32[]{:S(2)}) copy-start(f32[2,8,8,256]{3,2,1,0:T(8,128)} %get-tuple-element.7) | copy-start | bytes 393220
  132.2 2.3 %copy-start = (f32[256,256]{1,0:T(8,128)S(1)}, f32[256,256]{1,0:T(8,128)}, u32[]{:S(2)}) copy-start(f32[256,256]{1,0:T(8,128)} %get-tuple-element.14) | copy-start | bytes 786436

commit v3 on v2

--- a/solution.py
+++ b/solution.py
@@ -32,8 +32,8 @@
     feats_h, idxt_h, cnt_h, w_h, w1_h, w2_h, cot_h,
     out, gr1, gr2,
     feats, idxt, cnt, w, w1, w2, cot,
-    wtb, wr, wb, wf, stage, g1, oh, oht, pk, mine1, sum1, rc1, ab1, rp1, sw, g2,
-    mine2, sum2, rc2, ab2, rp2, bk, tt, pb, fr, nr, cb,
+    wtb, wr, wb, wf, stage, g1, oh, oht, pk, mine1, rc1, ab1, rp1, sw, g2,
+    mine2, rc2, ab2, rp2, bk, tt, pb, fr, nr, cb,
     in_s, sw_s, sw_r, wx_s, wx_r, z1_s, z1_r, c1_s, c1_r, p1_s, p1_r, sx_s, sx_r, z2_s, z2_r,
     c2_s, c2_r, p2_s, p2_r, ox_s, ox_r, bp_s, bp_r, bc_s, bc_r, fr_s, fr_r, nr_s, nr_r,
     *sums,
@@ -92,7 +92,7 @@
 
     alone = x == zb
     swap_r, swap_x = rid(y, za * 4 + x, core), zb
-    for m in range(1, 16):
+    for m in (1, 2, 3, 4, 12, 13, 14, 15):
         greet(zpeer(m), x)
     for m in range(1, 16):
         py, px, pr = peer(m)
@@ -112,19 +112,16 @@
 
     ins[2].wait()
     ins[3].wait()
-    row = iota((512, 512), 0)
-    plane, rest = row // 16, row % 16
-    source = (plane // 8) * 32 + (rest % 4) * 8 + plane % 8
-    order = one_hot((rest // 4) * 128 + source == iota((512, 512), 1))
+    row = iota((512, 1), 0)
+    plane, rest = row >> 4, row & 15
+    source = ((rest >> 2) << 7) + ((plane >> 3) << 5) + ((rest & 3) << 3) + (plane & 7)
+    order = one_hot(source == iota((512, 512), 1))
     for sq in range(4):
-        parts = []
-        for s4 in range(4):
-            s = sq * 4 + s4
-            parts.append(jnp.where(cnt[...] > x * 16 + s, w[:, s * 128:(s + 1) * 128].astype(F32), 0.0).astype(BF))
-        live = jnp.concatenate(parts, axis=1)
+        alive = [one_hot(cnt[...] > x * 16 + sq * 4 + s4) for s4 in range(4)]
+        live = w[:, sq * 512:(sq + 1) * 512] * jnp.concatenate(alive, axis=1)
         wtb[sq] = dot(order, live, 1, 1).astype(BF).reshape(32, 16, 256)
 
-    pl.semaphore_wait(barrier, 47 - alone.astype(jnp.int32))
+    pl.semaphore_wait(barrier, 40 - alone.astype(jnp.int32))
 
     def swap(src, dst, ssem, rsem):
         c = copy(src, dst, ssem, rsem, swap_r, swap_x)
@@ -163,10 +160,13 @@
     wr[me8, x] = wtb[:, q * 2 + core]
     yield "prep"
 
+    row, col = iota((256, 1), 0), iota((256, 256), 1)
+    regroup = one_hot(((row & 63) << 2) + (row >> 6) == col)
+    eye = one_hot(row == col)
     swap_done()
     yield "swap1"
 
-    def gather_z(g, rows, cut, ssem, rsem):
+    def gather_z(g, rows, cut, ssem, rsem, work):
         full, parts = pl.ds(0, rows), (pl.ds(0, cut), pl.ds(cut, rows - cut))
 
         def move(d, dist):
@@ -183,6 +183,7 @@
                 moves[d, dist] = move(d, dist)
                 moves[d, dist].start()
                 pending.append(moves[d, dist].wait_send)
+        work()
         for d in range(2):
             moves[d, 4].wait_recv()
             for dist in (8, 7, 6, 5):
@@ -193,7 +194,7 @@
             for d in range(2):
                 moves[d, dist].wait_recv()
 
-    gather_z(g1, 80, 48, z1_s, z1_r)
+    gather_z(g1, 80, 48, z1_s, z1_r, lambda: None)
     yield "gz1"
 
     ids = g1[:, 64:80, :].reshape(256, 128)
@@ -210,40 +211,41 @@
         c.wait_recv()
     yield "wwait"
 
-    row, col = iota((256, 256), 0), iota((256, 256), 1)
-    regroup = one_hot((row % 64) * 4 + row // 64 == col)
-    eye = one_hot(row == col)
 
     def weights(k):
         wb[k] = dot(regroup, wr[k].reshape(256, 256)).astype(BF)
         wf[k] = dot(eye, wb[k], 1, 1).astype(BF)
 
-    def reduce_planes(width, prepare, own, total, rc, ab, rp, csem_s, csem_r, psem_s, psem_r):
+    def reduce_planes(width, prepare, own, rc, ab, rp, csem_s, csem_r, psem_s, psem_r):
         def partial(k):
             prepare(k)
             picked = pk[:, pl.ds(pl.multiple_of(k * 64, 64), 64), 0:width].reshape(256, width)
             return dot(wf[k], picked)
 
+        near = (2, 1, 3, 0)
         cs = []
-        for j in range(4):
-            own[1, j] = partial(j * 2 + other).astype(BF)
-            cs.append(to_core(own.at[1, j], rc.at[j], csem_s.at[j], csem_r.at[j]))
-        for j in range(4):
-            total[j] = partial(j * 2 + core)
-        for j in range(4):
-            cs[j].wait_recv()
-            ab[j] = (total[j] + rc[j].astype(F32)).astype(BF).reshape(4, 64, width)
+        for off in near:
+            j = lax.rem(y + off, 4)
+            own[j] = partial(j * 2 + other).astype(BF)
+            cs.append(to_core(own.at[j], rc.at[j], csem_s.at[off], csem_r.at[off]))
         ps = []
-        for m in range(1, 16):
-            py, px, pr = peer(m)
-            ps.append(send(ab.at[py, px], rp.at[m], psem_s.at[m], psem_r.at[m], pr, px))
+        for n, off in enumerate(near):
+            j = lax.rem(y + off, 4)
+            mine_j = partial(j * 2 + core)
+            cs[n].wait_recv()
+            ab[j] = (mine_j + rc[j].astype(F32)).astype(BF).reshape(4, 64, width)
+            for mx in near:
+                m = off * 4 + mx
+                if m:
+                    px = lax.rem(x + mx, 4)
+                    ps.append((m, send(ab.at[j, px], rp.at[m], psem_s.at[m], psem_r.at[m], rid(j, z, core), px)))
         res = ab[y, x].astype(F32)
-        for m in range(1, 16):
-            ps[m - 1].wait_recv()
+        for m, c in ps[::-1]:
+            c.wait_recv()
             res = res + rp[m].astype(F32)
         return res.astype(BF)
 
-    sw[0] = reduce_planes(128, weights, mine1, sum1, rc1, ab1, rp1, c1_s, c1_r, p1_s, p1_r)
+    sw[0] = reduce_planes(128, weights, mine1, rc1, ab1, rp1, c1_s, c1_r, p1_s, p1_r)
     yield "red1"
     swap(sw.at[0], sw.at[1], sx_s, sx_r)()
     yield "swap2"
@@ -252,20 +254,29 @@
     agg1 = sw[1]
     z_one = dot(agg1, w1[...])
     g2[z] = (z_one * jax.nn.sigmoid(z_one)).astype(BF)
-    gather_z(g2, 64, 32, z2_s, z2_r)
+
+    def turn_picks():
+        for a in range(4):
+            oht[a] = dot(eye, oh[a], 1, 1).astype(BF)
+
+    gather_z(g2, 64, 32, z2_s, z2_r, turn_picks)
     yield "gz2"
     for a in range(4):
         pk[a] = dot(oh[a], g2[4 * a:4 * a + 4].reshape(256, 256)).astype(BF)
-    agg2 = reduce_planes(256, lambda k: None, mine2, sum2, rc2, ab2, rp2, c2_s, c2_r, p2_s, p2_r)
+    agg2 = reduce_planes(256, lambda k: None, mine2, rc2, ab2, rp2, c2_s, c2_r, p2_s, p2_r)
     yield "red2"
 
     z_two = dot(agg2, w2[...])
     dz2 = (cot[mine, :].astype(F32) * silu_slope(z_two)).astype(BF)
     bk[y, core, mine, :] = dot(dz2, w2[...], 1, 1).astype(BF)
-    bcopies = []
-    for m in range(1, 16):
-        py, px, pr = peer(m)
-        bcopies.append(send(bk.at[y, core, mine], bk.at[y, core, mine], bp_s.at[m], bp_r.at[m], pr, px))
+    bcopies = {}
+    for off in (2, 1, 3, 0):
+        for mx in (2, 1, 3, 0):
+            m = off * 4 + mx
+            if m:
+                py, px = lax.rem(y + off, 4), lax.rem(x + mx, 4)
+                bcopies[m] = send(bk.at[y, core, mine], bk.at[y, core, mine], bp_s.at[m], bp_r.at[m],
+                                  rid(py, z, core), px)
     out[mine, :] = (z_two * jax.nn.sigmoid(z_two)).astype(BF)
     ocopies = []
     for m in range(1, 4):
@@ -285,17 +296,18 @@
         for m in range(1, 16):
             ps[m - 1].wait_recv()
             total = total + gp[m]
-        gz[0] = total
+        wide = gz.dtype == BF
+        gz[0] = jnp.concatenate([total[:, :128], total[:, 128:]], axis=0).astype(BF) if wide else total
         zs = []
         for m in (8, 7, 9, 6, 10, 5, 11, 4, 12, 3, 13, 2, 14, 1, 15):
             zs.append(send(gz.at[0], gz.at[m], z_s.at[m], z_r.at[m], zpeer(m), x))
         yield
         for c in zs:
             c.wait_recv()
-        total = jnp.zeros_like(total)
-        for k in range(16):
-            total = total + gz[lax.rem(z - k + 16, 16)]
-        gt[core, q] = total
+        total = gz[z].astype(F32)
+        for k in range(1, 16):
+            total = total + gz[lax.rem(z - k + 16, 16)].astype(F32)
+        gt[core, q] = jnp.concatenate([total[:8], total[8:]], axis=1) if wide else total
         ts = []
         for m in range(1, 16):
             py, px, pr = peer(m)
@@ -314,22 +326,24 @@
     ga2[...] = dot(agg2, dz2, 0, 0).reshape(2, 16, 8, 256)
     next(reduce2)
 
-    for a in range(4):
-        oht[a] = dot(eye, oh[a], 1, 1).astype(BF)
-    for c in bcopies:
-        c.wait_recv()
-    cc = [to_core(bk.at[j, core], bk.at[j, core], bc_s.at[j], bc_r.at[j]) for j in range(4)]
-    next(reduce2)
 
     def slot_terms(k):
         got = dot(wb[k], bk[lax.div(k, 2), lax.rem(k, 2)]).astype(BF)
         tt[:, pl.ds(pl.multiple_of(k * 64, 64), 64), :] = got.reshape(4, 64, 256)
 
-    for j in range(4):
+    next(reduce2)
+    cc = {}
+    for off in (0, 1, 3, 2):
+        j = lax.rem(y - off + 4, 4)
+        for mx in range(4):
+            if off * 4 + mx:
+                bcopies[off * 4 + mx].wait_recv()
+        cc[off] = to_core(bk.at[j, core], bk.at[j, core], bc_s.at[off], bc_r.at[off])
         slot_terms(j * 2 + core)
-    for j in range(4):
-        cc[j].wait_recv()
-        slot_terms(j * 2 + other)
+    next(reduce2)
+    for off in (0, 1, 3, 2):
+        cc[off].wait_recv()
+        slot_terms(lax.rem(y - off + 4, 4) * 2 + other)
     yield "bwait"
     for a in range(4):
         pb[4 * a:4 * a + 4] = dot(oht[a], tt[a]).astype(BF).reshape(4, 64, 256)
@@ -346,7 +360,6 @@
         for d in range(2):
             sign = 1 if d == 0 else -1
             nears[d, m] = send(pb.at[zat(sign * m)], nr.at[d, m], nr_s.at[d, m], nr_r.at[d, m], zpeer(sign * m), x)
-    next(reduce2)
     for d in range(2):
         sign = 1 if d == 0 else -1
         acc = pb[zat(sign * 4)].astype(F32)
@@ -420,15 +433,13 @@
         vmem(BF, 4, 512, 256),
         vmem(BF, 4, 256, 512),
         vmem(BF, 4, 512, 256),
-        vmem(BF, 2, 4, 256, 128),
-        vmem(F32, 4, 256, 128),
+        vmem(BF, 4, 256, 128),
         vmem(BF, 4, 256, 128),
         vmem(BF, 4, 4, 64, 128),
         vmem(BF, 16, 64, 128),
         vmem(BF, 2, 64, 128),
         vmem(BF, 16, 64, 256),
-        vmem(BF, 2, 4, 256, 256),
-        vmem(F32, 4, 256, 256),
+        vmem(BF, 4, 256, 256),
         vmem(BF, 4, 256, 256),
         vmem(BF, 4, 4, 64, 256),
         vmem(BF, 16, 64, 256),
@@ -449,7 +460,7 @@
             vmem(F32, 16, 8, width),
             vmem(F32, 16, 8, width),
             vmem(F32, 16, 8, width),
-            vmem(F32, 16, 8, width),
+            vmem(BF, 16, 16, 128) if width == 256 else vmem(F32, 16, 8, width),
             vmem(F32, 2, 16, 8, width),
             dma(()), dma(()), dma((16,)), dma((16,)), dma((16,)), dma((16,)), dma((16,)), dma((16,)), dma(()), dma(()),
         ]

time: 135 us -> 128 us (0.948)
  Pallas kernels: 132 us -> 124 us
    pallas_call x1, Pallas kernels: 132 us -> 124 us  [local(): pl.pallas_call(kernel, out_shape=(jax.ShapeDtypeStruct((256, 256), BF), j...]
where the time goes in v3:
time: 128 us
  Pallas kernels  124 us (97%)
  local copies, waits for them, and re-layouts  2.98 us (2%)
    pallas_call x1, Pallas kernels, local(): pl.pallas_call(kernel, out_shape=(jax.ShapeDtypeStruct((256, 256), BF), j...  124 us
    unnamed x7, local copies, waits for them, and re-layouts  2.98 us

profile of v3, /device:TPU:1, one launch (start us, length us, event | category | flops | bytes accessed | tf_op | source)
XLA Modules:
  0.0 128.0 jit_solution(3443062880991462890)
XLA Ops:
  0.6 124.4 %shard_map.94 = (bf16[256,256]{1,0:T(8,128)(2,1)}, f32[2,8,8,256]{3,2,1,0:T(8,128)}, f32[256,256]{1,0:T(8,128)}) custom-call(bf16[256,128]{1,0:T(8,128)(2,1)} %refs_0_.1, s32[16,128]{1,0:T(8,128)} %bitcast.5, s32[1,128]{1,0:T(1,128)} %refs_2_.1, bf16[256,2048]{1,0:T(8,128)(2,1)} %refs_3_.1, bf16[128,256]{1,0:T(8,128)(2,1)} %refs_4_.1, ...), custom_call_target="tpu_custom_call" | custom-call | tf_op jit(solution)/shard_map/pallas_call | solution.py:467
  125.0 0.0 copy-start.1
  125.0 0.0 copy-start
  125.0 1.6 %copy.13 = bf16[256,256]{1,0:T(8,128)(2,1)} copy(bf16[256,256]{1,0:T(8,128)(2,1)} %get-tuple-element.12) | data formatting | bytes 262144
  126.7 0.0 copy-done.1
  126.7 0.7 copy.14
  127.3 0.0 copy-done
  127.3 0.7 copy.15
Async XLA Ops:
  125.0 1.6 %copy-start.1 = (f32[2,8,8,256]{3,2,1,0:T(8,128)S(1)}, f32[2,8,8,256]{3,2,1,0:T(8,128)}, u32[]{:S(2)}) copy-start(f32[2,8,8,256]{3,2,1,0:T(8,128)} %get-tuple-element.7) | copy-start | bytes 393220
  125.0 2.3 %copy-start = (f32[256,256]{1,0:T(8,128)S(1)}, f32[256,256]{1,0:T(8,128)}, u32[]{:S(2)}) copy-start(f32[256,256]{1,0:T(8,128)} %get-tuple-element.14) | copy-start | bytes 786436

commit v4 on v3

--- a/solution.py
+++ b/solution.py
@@ -35,7 +35,7 @@
     wtb, wr, wb, wf, stage, g1, oh, oht, pk, mine1, rc1, ab1, rp1, sw, g2,
     mine2, rc2, ab2, rp2, bk, tt, pb, fr, nr, cb,
     in_s, sw_s, sw_r, wx_s, wx_r, z1_s, z1_r, c1_s, c1_r, p1_s, p1_r, sx_s, sx_r, z2_s, z2_r,
-    c2_s, c2_r, p2_s, p2_r, ox_s, ox_r, bp_s, bp_r, bc_s, bc_r, fr_s, fr_r, nr_s, nr_r,
+    c2_s, c2_r, p2_s, p2_r, ox_s, ox_r, bp_s, bp_r, bc_s, bc_r, fr_s, fr_r,
     *sums,
 ):
     r = lax.axis_index("rows")
@@ -119,7 +119,7 @@
     for sq in range(4):
         alive = [one_hot(cnt[...] > x * 16 + sq * 4 + s4) for s4 in range(4)]
         live = w[:, sq * 512:(sq + 1) * 512] * jnp.concatenate(alive, axis=1)
-        wtb[sq] = dot(order, live, 1, 1).astype(BF).reshape(32, 16, 256)
+        wtb[:, sq] = dot(order, live, 1, 1).astype(BF).reshape(32, 16, 256)
 
     pl.semaphore_wait(barrier, 40 - alone.astype(jnp.int32))
 
@@ -149,15 +149,17 @@
 
     swap_done = swap(stage, g1.at[za * 4 + x], sw_s, sw_r)
 
-    wcopies = []
+    wcopies = {}
     me8 = y * 2 + core
-    for m in range(1, 16):
-        py, px, pr = peer(m)
-        for h, hr in ((core, pr), (other, rid(py, z, other))):
-            n = 2 * m + (0 if h is core else 1)
-            wcopies.append(send(wtb.at[:, (py * 4 + px) * 2 + h], wr.at[me8, x], wx_s.at[n], wx_r.at[n], hr, px))
-    wcopies.append(to_core(wtb.at[:, q * 2 + other], wr.at[me8, x], wx_s.at[1], wx_r.at[1]))
-    wr[me8, x] = wtb[:, q * 2 + core]
+    for off in (2, 1, 3, 0):
+        for mx in (2, 1, 3, 0):
+            py, px = lax.rem(y + off, 4), lax.rem(x + mx, 4)
+            for n, h in enumerate((core, other)):
+                m = (off * 4 + mx) * 2 + n
+                if m:
+                    wcopies[m] = send(wtb.at[(py * 4 + px) * 2 + h], wr.at[me8, x], wx_s.at[m], wx_r.at[m],
+                                      rid(py, z, h), px)
+    wr[me8, x] = wtb[q * 2 + core]
     yield "prep"
 
     row, col = iota((256, 1), 0), iota((256, 256), 1)
@@ -169,28 +171,29 @@
     def gather_z(g, rows, cut, ssem, rsem, work):
         full, parts = pl.ds(0, rows), (pl.ds(0, cut), pl.ds(cut, rows - cut))
 
-        def move(d, dist):
-            sign = 1 if d == 0 else -1
-            far = dist > 4
-            part = parts[d] if dist == 8 else full
-            slot = zat(-sign * 4) if far else z
-            return copy(g.at[slot, part], g.at[slot, part], ssem.at[d, dist], rsem.at[d, dist],
-                        zpeer(sign * (dist - 4 if far else dist)), x)
-
         moves = {}
-        for dist in (4, 3, 2, 1):
+
+        def move(dist, via):
             for d in range(2):
-                moves[d, dist] = move(d, dist)
-                moves[d, dist].start()
-                pending.append(moves[d, dist].wait_send)
+                sign = 1 if d == 0 else -1
+                if via:
+                    moves[d, via].wait_recv()
+                part = parts[d] if dist == 8 else full
+                piece = g.at[zat(-sign * via), part]
+                moves[d, dist] = send(piece, piece, ssem.at[d, dist], rsem.at[d, dist], zpeer(sign * (dist - via)), x)
+                for more in (8, 5) if dist == 6 else ():
+                    part = parts[d] if more == 8 else full
+                    piece = g.at[zat(-sign * via), part]
+                    moves[d, more] = send(piece, piece, ssem.at[d, more], rsem.at[d, more],
+                                          zpeer(sign * (more - via)), x)
+
+        for dist in (4, 2, 1):
+            move(dist, 0)
         work()
-        for d in range(2):
-            moves[d, 4].wait_recv()
-            for dist in (8, 7, 6, 5):
-                moves[d, dist] = move(d, dist)
-                moves[d, dist].start()
-                pending.append(moves[d, dist].wait_send)
-        for dist in (1, 2, 3, 5, 6, 7, 8):
+        move(3, 2)
+        move(6, 4)
+        move(7, 6)
+        for dist in (1, 3, 5, 8, 7):
             for d in range(2):
                 moves[d, dist].wait_recv()
 
@@ -207,18 +210,20 @@
         pk[a, :, 0:128] = dot(oh[a], g1[4 * a:4 * a + 4, 0:64, :].reshape(256, 128)).astype(BF)
 
     yield "picks1"
-    for c in wcopies:
-        c.wait_recv()
-    yield "wwait"
-
-
-    def weights(k):
+
+
+    def weights(k, off, n):
+        for mx in range(4):
+            m = ((4 - off) % 4 * 4 + mx) * 2 + n
+            if m:
+                wcopies[m].wait_recv()
         wb[k] = dot(regroup, wr[k].reshape(256, 256)).astype(BF)
         wf[k] = dot(eye, wb[k], 1, 1).astype(BF)
 
     def reduce_planes(width, prepare, own, rc, ab, rp, csem_s, csem_r, psem_s, psem_r):
-        def partial(k):
-            prepare(k)
+        def partial(j, off, n):
+            k = j * 2 + (other if n else core)
+            prepare(k, off, n)
             picked = pk[:, pl.ds(pl.multiple_of(k * 64, 64), 64), 0:width].reshape(256, width)
             return dot(wf[k], picked)
 
@@ -226,12 +231,12 @@
         cs = []
         for off in near:
             j = lax.rem(y + off, 4)
-            own[j] = partial(j * 2 + other).astype(BF)
+            own[j] = partial(j, off, 1).astype(BF)
             cs.append(to_core(own.at[j], rc.at[j], csem_s.at[off], csem_r.at[off]))
         ps = []
         for n, off in enumerate(near):
             j = lax.rem(y + off, 4)
-            mine_j = partial(j * 2 + core)
+            mine_j = partial(j, off, 0)
             cs[n].wait_recv()
             ab[j] = (mine_j + rc[j].astype(F32)).astype(BF).reshape(4, 64, width)
             for mx in near:
@@ -263,7 +268,7 @@
     yield "gz2"
     for a in range(4):
         pk[a] = dot(oh[a], g2[4 * a:4 * a + 4].reshape(256, 256)).astype(BF)
-    agg2 = reduce_planes(256, lambda k: None, mine2, rc2, ab2, rp2, c2_s, c2_r, p2_s, p2_r)
+    agg2 = reduce_planes(256, lambda k, off, n: None, mine2, rc2, ab2, rp2, c2_s, c2_r, p2_s, p2_r)
     yield "red2"
 
     z_two = dot(agg2, w2[...])
@@ -349,34 +354,37 @@
         pb[4 * a:4 * a + 4] = dot(oht[a], tt[a]).astype(BF).reshape(4, 64, 256)
 
     full, parts = pl.ds(0, 64), (pl.ds(0, 32), pl.ds(32, 32))
-    fars, nears = {}, {}
-    for m in (4, 3, 2, 1):
-        for d in range(2):
-            sign = 1 if d == 0 else -1
-            part = parts[d] if m == 4 else full
-            fars[d, m] = send(pb.at[zat(sign * (4 + m)), part], fr.at[d, m, part], fr_s.at[d, m], fr_r.at[d, m],
-                              zpeer(sign * m), x)
-    for m in (3, 2, 1):
-        for d in range(2):
-            sign = 1 if d == 0 else -1
-            nears[d, m] = send(pb.at[zat(sign * m)], nr.at[d, m], nr_s.at[d, m], nr_r.at[d, m], zpeer(sign * m), x)
-    for d in range(2):
-        sign = 1 if d == 0 else -1
-        acc = pb[zat(sign * 4)].astype(F32)
-        for m in (1, 2, 3):
-            fars[d, m].wait_recv()
-            acc = acc + fr[d, m].astype(F32)
-        fars[d, 4].wait_recv()
-        cb[d] = acc.astype(BF)
+    ways = ((0, 1), (1, -1))
+    moves = {}
+
+    def pass_on(d, sign, dist, src, slot, hop, part=full):
+        dst = fr.at[d, slot, part] if slot < 5 else nr.at[d, slot - 5]
+        moves[d, dist] = send(src, dst, fr_s.at[d, dist], fr_r.at[d, dist], zpeer(sign * hop), x)
+
+    for dist, slot, hop in ((7, 0, 1), (8, 3, 4), (5, 1, 1), (3, 4, 1), (1, 5, 1)):
+        for d, sign in ways:
+            part = parts[d] if dist == 8 else full
+            pass_on(d, sign, dist, pb.at[zat(sign * dist), part], slot, hop, part)
+    for dist, via, slot, out_slot in ((6, 7, 0, 2), (2, 3, 4, 6)):
+        for d, sign in ways:
+            moves[d, via].wait_recv()
+            cb[d, dist // 2] = (pb[zat(sign * dist)].astype(F32) + fr[d, slot].astype(F32)).astype(BF)
+            pass_on(d, sign, dist, cb.at[d, dist // 2], out_slot, 2)
+    for d, sign in ways:
+        moves[d, 5].wait_recv()
+        moves[d, 6].wait_recv()
+        acc = pb[zat(sign * 4)].astype(F32) + fr[d, 1].astype(F32) + fr[d, 2].astype(F32)
+        moves[d, 8].wait_recv()
+        cb[d, 2] = acc.astype(BF)
         lo = 0 if d == 0 else 32
-        cb[d, lo:lo + 32, :] = (acc[lo:lo + 32] + fr[d, 4, lo:lo + 32, :].astype(F32)).astype(BF)
-        nears[d, 4] = send(cb.at[d], nr.at[d, 4], nr_s.at[d, 4], nr_r.at[d, 4], zpeer(sign * 4), x)
+        cb[d, 2, lo:lo + 32, :] = (acc[lo:lo + 32] + fr[d, 3, lo:lo + 32, :].astype(F32)).astype(BF)
+        pass_on(d, sign, 4, cb.at[d, 2], 7, 4)
     next(reduce2)
     dh = pb[z].astype(F32)
-    for m in (1, 2, 3, 4):
+    for dist, slot in ((1, 0), (2, 1), (4, 2)):
         for d in range(2):
-            nears[d, m].wait_recv()
-            dh = dh + nr[d, m].astype(F32)
+            moves[d, dist].wait_recv()
+            dh = dh + nr[d, slot].astype(F32)
     yield "rsz"
     dz1 = (dh * silu_slope(z_one)).astype(BF)
     grad1 = dot(agg1, dz1, 0, 0).reshape(2, 8, 8, 256)
@@ -413,6 +421,14 @@
         wait()
 
 
+def place(*refs):
+    copies = [pltpu.make_async_copy(refs[n], refs[3 + n], refs[6].at[n]) for n in range(3)]
+    for c in copies:
+        c.start()
+    for c in copies:
+        c.wait()
+
+
 def local(feats, edge_w, send_rows, counts, w_one, w_two, cotangent):
     idxt = jnp.transpose(send_rows[0])
     vm = pl.BlockSpec(memory_space=pltpu.VMEM)
@@ -424,7 +440,7 @@
         return pltpu.VMEM(shape, kind)
 
     scratch = [pltpu.VMEM(a.shape, a.dtype) for a in args] + [
-        vmem(BF, 4, 32, 16, 256),
+        vmem(BF, 32, 4, 16, 256),
         vmem(BF, 8, 4, 4, 16, 256),
         vmem(BF, 8, 256, 256),
         vmem(BF, 8, 256, 256),
@@ -447,12 +463,12 @@
         vmem(BF, 4, 512, 256),
         vmem(BF, 16, 64, 256),
         vmem(BF, 2, 5, 64, 256),
-        vmem(BF, 2, 5, 64, 256),
-        vmem(BF, 2, 64, 256),
+        vmem(BF, 2, 3, 64, 256),
+        vmem(BF, 2, 4, 64, 256),
         dma((7,)), dma(()), dma(()), dma((32,)), dma((32,)), dma((2, 9)), dma((2, 9)),
         dma((4,)), dma((4,)), dma((16,)), dma((16,)), dma(()), dma(()), dma((2, 9)), dma((2, 9)),
         dma((4,)), dma((4,)), dma((16,)), dma((16,)), dma((4,)), dma((4,)), dma((16,)), dma((16,)),
-        dma((4,)), dma((4,)), dma((2, 5)), dma((2, 5)), dma((2, 5)), dma((2, 5)),
+        dma((4,)), dma((4,)), dma((2, 9)), dma((2, 9)),
     ]
     for width, first in ((256, (2, 16, 8, 256)), (128, (2, 8, 2, 8, 128))):
         scratch += [
@@ -478,7 +494,17 @@
             collective_id=0, has_side_effects=True, vmem_limit_bytes=56 * 1024 * 1024
         ),
     )(*args)
-    return out, gr1.reshape(128, 256), gr2
+    return pl.pallas_call(
+        place,
+        out_shape=(
+            jax.ShapeDtypeStruct((256, 256), BF),
+            jax.ShapeDtypeStruct((128, 256), F32),
+            jax.ShapeDtypeStruct((256, 256), F32),
+        ),
+        in_specs=[hbm] * 3,
+        out_specs=(hbm, hbm, hbm),
+        scratch_shapes=[dma((3,))],
+    )(out, gr1.reshape(128, 256), gr2)
 
 
 def solution(mesh):

time: 128 us -> 142 us (1.11)
  Pallas kernels: 124 us -> 142 us
  local copies, waits for them, and re-layouts: 2.98 us -> 0 us
    pallas_call x0 -> x1, Pallas kernels: none -> 17 us  [local(): pl.pallas_call(place, out_shape=(jax.ShapeDtypeStruct((256, 256), BF), ja...]
    unnamed x7 -> x0, local copies, waits for them, and re-layouts: 2.98 us -> none
where the time goes in v4:
time: 142 us
  Pallas kernels  142 us (100%)
    pallas_call x1, Pallas kernels, local(): pl.pallas_call(kernel, out_shape=(jax.ShapeDtypeStruct((256, 256), BF), j...  125 us
    pallas_call x1, Pallas kernels, local(): pl.pallas_call(place, out_shape=(jax.ShapeDtypeStruct((256, 256), BF), ja...  17 us

profile of v4, /device:TPU:1, one launch (start us, length us, event | category | flops | bytes accessed | tf_op | source)
XLA Modules:
  0.0 142.2 jit_solution(11320799263770070748)
XLA Ops:
  0.6 124.5 %shard_map.94 = (bf16[256,256]{1,0:T(8,128)(2,1)}, f32[2,8,8,256]{3,2,1,0:T(8,128)}, f32[256,256]{1,0:T(8,128)}) custom-call(bf16[256,128]{1,0:T(8,128)(2,1)} %refs_0_.1, s32[16,128]{1,0:T(8,128)} %bitcast.5, s32[1,128]{1,0:T(1,128)} %refs_2_.1, bf16[256,2048]{1,0:T(8,128)(2,1)} %refs_3_.1, bf16[128,256]{1,0:T(8,128)(2,1)} %refs_4_.1, ...), custom_call_target="tpu_custom_call" | custom-call | tf_op jit(solution)/shard_map/pallas_call | solution.py:483
  125.2 17.0 %shard_map.95 = (bf16[256,256]{1,0:T(8,128)(2,1)}, f32[128,256]{1,0:T(8,128)}, f32[256,256]{1,0:T(8,128)}) custom-call(bf16[256,256]{1,0:T(8,128)(2,1)} %get-tuple-element.6.refs_0_, f32[128,256]{1,0:T(8,128)} %bitcast.4, f32[256,256]{1,0:T(8,128)} %get-tuple-element.8.refs_2_), custom_call_target="tpu_custom_call" | custom-call | tf_op jit(solution)/shard_map/pallas_call | solution.py:497

commit v5 on v3

--- a/solution.py
+++ b/solution.py
@@ -21,6 +21,14 @@
 
 def iota(shape, dim):
     return lax.broadcasted_iota(jnp.int32, shape, dim)
+
+
+def each(lo, hi, fn):
+    def step(n, carry):
+        fn(n)
+        return carry
+
+    lax.fori_loop(lo, hi, step, 0)
 
 
 def one_hot(hit):
@@ -74,6 +82,13 @@
         pending.append(c.wait_send)
         return c
 
+    def start_all(lo, hi, make):
+        each(lo, hi, lambda m: make(m).start())
+        pending.append(lambda: each(lo, hi, lambda m: make(m).wait_send()))
+
+    def rel(m):
+        return lax.rem(y + lax.div(m, 4), 4), lax.rem(x + lax.rem(m, 4), 4)
+
     def to_core(src, dst, ssem, rsem):
         return send(src, dst, ssem, rsem, rid(y, z, other), x)
 
@@ -116,11 +131,12 @@
     plane, rest = row >> 4, row & 15
     source = ((rest >> 2) << 7) + ((plane >> 3) << 5) + ((rest & 3) << 3) + (plane & 7)
     order = one_hot(source == iota((512, 512), 1))
-    for sq in range(4):
+    def regroup_weights(sq):
         alive = [one_hot(cnt[...] > x * 16 + sq * 4 + s4) for s4 in range(4)]
-        live = w[:, sq * 512:(sq + 1) * 512] * jnp.concatenate(alive, axis=1)
-        wtb[sq] = dot(order, live, 1, 1).astype(BF).reshape(32, 16, 256)
-
+        live = w[:, pl.ds(pl.multiple_of(sq * 512, 512), 512)] * jnp.concatenate(alive, axis=1)
+        wtb[:, sq] = dot(order, live, 1, 1).astype(BF).reshape(32, 16, 256)
+
+    each(0, 4, regroup_weights)
     pl.semaphore_wait(barrier, 40 - alone.astype(jnp.int32))
 
     def swap(src, dst, ssem, rsem):
@@ -149,15 +165,15 @@
 
     swap_done = swap(stage, g1.at[za * 4 + x], sw_s, sw_r)
 
-    wcopies = []
     me8 = y * 2 + core
-    for m in range(1, 16):
-        py, px, pr = peer(m)
-        for h, hr in ((core, pr), (other, rid(py, z, other))):
-            n = 2 * m + (0 if h is core else 1)
-            wcopies.append(send(wtb.at[:, (py * 4 + px) * 2 + h], wr.at[me8, x], wx_s.at[n], wx_r.at[n], hr, px))
-    wcopies.append(to_core(wtb.at[:, q * 2 + other], wr.at[me8, x], wx_s.at[1], wx_r.at[1]))
-    wr[me8, x] = wtb[:, q * 2 + core]
+
+    def weight_copy(m):
+        py, px = rel(lax.div(m, 2))
+        h = lax.rem(core + lax.rem(m, 2), 2)
+        return copy(wtb.at[(py * 4 + px) * 2 + h], wr.at[me8, x], wx_s.at[m], wx_r.at[m], rid(py, z, h), px)
+
+    start_all(1, 32, weight_copy)
+    wr[me8, x] = wtb[q * 2 + core]
     yield "prep"
 
     row, col = iota((256, 1), 0), iota((256, 256), 1)
@@ -169,28 +185,29 @@
     def gather_z(g, rows, cut, ssem, rsem, work):
         full, parts = pl.ds(0, rows), (pl.ds(0, cut), pl.ds(cut, rows - cut))
 
-        def move(d, dist):
-            sign = 1 if d == 0 else -1
-            far = dist > 4
-            part = parts[d] if dist == 8 else full
-            slot = zat(-sign * 4) if far else z
-            return copy(g.at[slot, part], g.at[slot, part], ssem.at[d, dist], rsem.at[d, dist],
-                        zpeer(sign * (dist - 4 if far else dist)), x)
-
         moves = {}
-        for dist in (4, 3, 2, 1):
+
+        def move(dist, via):
             for d in range(2):
-                moves[d, dist] = move(d, dist)
-                moves[d, dist].start()
-                pending.append(moves[d, dist].wait_send)
+                sign = 1 if d == 0 else -1
+                if via:
+                    moves[d, via].wait_recv()
+                part = parts[d] if dist == 8 else full
+                piece = g.at[zat(-sign * via), part]
+                moves[d, dist] = send(piece, piece, ssem.at[d, dist], rsem.at[d, dist], zpeer(sign * (dist - via)), x)
+                for more in (8, 5) if dist == 6 else ():
+                    part = parts[d] if more == 8 else full
+                    piece = g.at[zat(-sign * via), part]
+                    moves[d, more] = send(piece, piece, ssem.at[d, more], rsem.at[d, more],
+                                          zpeer(sign * (more - via)), x)
+
+        for dist in (4, 2, 1):
+            move(dist, 0)
         work()
-        for d in range(2):
-            moves[d, 4].wait_recv()
-            for dist in (8, 7, 6, 5):
-                moves[d, dist] = move(d, dist)
-                moves[d, dist].start()
-                pending.append(moves[d, dist].wait_send)
-        for dist in (1, 2, 3, 5, 6, 7, 8):
+        move(3, 2)
+        move(6, 4)
+        move(7, 6)
+        for dist in (1, 3, 5, 8, 7):
             for d in range(2):
                 moves[d, dist].wait_recv()
 
@@ -199,51 +216,77 @@
 
     ids = g1[:, 64:80, :].reshape(256, 128)
     lane = iota((256, 256), 1).astype(F32)
-    for k in range(8):
-        at = ((k // 2) * 16 + z) * 2 + k % 2
+
+    def pick_rows(k):
+        at = (lax.div(k, 2) * 16 + z) * 2 + lax.rem(k, 2)
         rows = dot(ids, one_hot(iota((128, 256), 0) == at))
-        oh[:, k * 64:(k + 1) * 64, :] = one_hot(rows == lane).reshape(4, 64, 256)
-    for a in range(4):
-        pk[a, :, 0:128] = dot(oh[a], g1[4 * a:4 * a + 4, 0:64, :].reshape(256, 128)).astype(BF)
-
+        oh[:, pl.ds(pl.multiple_of(k * 64, 64), 64), :] = one_hot(rows == lane).reshape(4, 64, 256)
+
+    each(0, 8, pick_rows)
+
+    def pick1(a):
+        pk[a, :, 0:128] = dot(oh[a], g1[pl.ds(a * 4, 4), 0:64, :].reshape(256, 128)).astype(BF)
+
+    each(0, 4, pick1)
     yield "picks1"
-    for c in wcopies:
-        c.wait_recv()
-    yield "wwait"
-
-
-    def weights(k):
+
+
+    def weights(k, off, n):
+        def arrived(mx):
+            m = (lax.rem(4 - off, 4) * 4 + mx) * 2 + n
+
+            @pl.when(m > 0)
+            def _():
+                weight_copy(m).wait_recv()
+
+        each(0, 4, arrived)
         wb[k] = dot(regroup, wr[k].reshape(256, 256)).astype(BF)
         wf[k] = dot(eye, wb[k], 1, 1).astype(BF)
 
     def reduce_planes(width, prepare, own, rc, ab, rp, csem_s, csem_r, psem_s, psem_r):
-        def partial(k):
-            prepare(k)
+        def partial(j, off, n):
+            k = j * 2 + (other if n else core)
+            prepare(k, off, n)
             picked = pk[:, pl.ds(pl.multiple_of(k * 64, 64), 64), 0:width].reshape(256, width)
             return dot(wf[k], picked)
 
-        near = (2, 1, 3, 0)
-        cs = []
-        for off in near:
+        def swap_half(n):
+            off = lax.rem(n + 2, 4)
             j = lax.rem(y + off, 4)
-            own[j] = partial(j * 2 + other).astype(BF)
-            cs.append(to_core(own.at[j], rc.at[j], csem_s.at[off], csem_r.at[off]))
-        ps = []
-        for n, off in enumerate(near):
-            j = lax.rem(y + off, 4)
-            mine_j = partial(j * 2 + core)
-            cs[n].wait_recv()
+            return off, j, copy(own.at[j], rc.at[j], csem_s.at[off], csem_r.at[off], rid(y, z, other), x)
+
+        def other_half(n):
+            off, j, c = swap_half(n)
+            own[j] = partial(j, off, 1).astype(BF)
+            c.start()
+
+        each(0, 4, other_half)
+        pending.append(lambda: each(0, 4, lambda n: swap_half(n)[2].wait_send()))
+
+        def piece(m):
+            py, px = rel(m)
+            return copy(ab.at[py, px], rp.at[m], psem_s.at[m], psem_r.at[m], rid(py, z, core), px)
+
+        def own_half(n):
+            off, j, c = swap_half(n)
+            mine_j = partial(j, off, 0)
+            c.wait_recv()
             ab[j] = (mine_j + rc[j].astype(F32)).astype(BF).reshape(4, 64, width)
-            for mx in near:
-                m = off * 4 + mx
-                if m:
-                    px = lax.rem(x + mx, 4)
-                    ps.append((m, send(ab.at[j, px], rp.at[m], psem_s.at[m], psem_r.at[m], rid(j, z, core), px)))
-        res = ab[y, x].astype(F32)
-        for m, c in ps[::-1]:
-            c.wait_recv()
-            res = res + rp[m].astype(F32)
-        return res.astype(BF)
+            for mx in (2, 1, 3):
+                piece(off * 4 + mx).start()
+
+            @pl.when(off > 0)
+            def _():
+                piece(off * 4).start()
+
+        each(0, 4, own_half)
+        pending.append(lambda: each(1, 16, lambda m: piece(m).wait_send()))
+
+        def add(m, res):
+            piece(m).wait_recv()
+            return res + rp[m].astype(F32)
+
+        return lax.fori_loop(1, 16, add, ab[y, x].astype(F32)).astype(BF)
 
     sw[0] = reduce_planes(128, weights, mine1, rc1, ab1, rp1, c1_s, c1_r, p1_s, p1_r)
     yield "red1"
@@ -256,27 +299,30 @@
     g2[z] = (z_one * jax.nn.sigmoid(z_one)).astype(BF)
 
     def turn_picks():
-        for a in range(4):
+        def turn(a):
             oht[a] = dot(eye, oh[a], 1, 1).astype(BF)
+
+        each(0, 4, turn)
 
     gather_z(g2, 64, 32, z2_s, z2_r, turn_picks)
     yield "gz2"
-    for a in range(4):
-        pk[a] = dot(oh[a], g2[4 * a:4 * a + 4].reshape(256, 256)).astype(BF)
-    agg2 = reduce_planes(256, lambda k: None, mine2, rc2, ab2, rp2, c2_s, c2_r, p2_s, p2_r)
+
+    def pick2(a):
+        pk[a] = dot(oh[a], g2[pl.ds(a * 4, 4)].reshape(256, 256)).astype(BF)
+
+    each(0, 4, pick2)
+    agg2 = reduce_planes(256, lambda k, off, n: None, mine2, rc2, ab2, rp2, c2_s, c2_r, p2_s, p2_r)
     yield "red2"
 
     z_two = dot(agg2, w2[...])
     dz2 = (cot[mine, :].astype(F32) * silu_slope(z_two)).astype(BF)
     bk[y, core, mine, :] = dot(dz2, w2[...], 1, 1).astype(BF)
-    bcopies = {}
-    for off in (2, 1, 3, 0):
-        for mx in (2, 1, 3, 0):
-            m = off * 4 + mx
-            if m:
-                py, px = lax.rem(y + off, 4), lax.rem(x + mx, 4)
-                bcopies[m] = send(bk.at[y, core, mine], bk.at[y, core, mine], bp_s.at[m], bp_r.at[m],
-                                  rid(py, z, core), px)
+
+    def back_copy(m):
+        py, px = rel(m)
+        return copy(bk.at[y, core, mine], bk.at[y, core, mine], bp_s.at[m], bp_r.at[m], rid(py, z, core), px)
+
+    start_all(1, 16, back_copy)
     out[mine, :] = (z_two * jax.nn.sigmoid(z_two)).astype(BF)
     ocopies = []
     for m in range(1, 4):
@@ -287,34 +333,41 @@
         yield
         c.wait_recv()
         gs[...] = ga[core] + rc[...]
-        ps = []
-        for m in range(1, 16):
-            py, px, pr = peer(m)
-            ps.append(send(gs.at[py * 4 + px], gp.at[m], p_s.at[m], p_r.at[m], pr, px))
+
+        def part(m):
+            py, px = rel(m)
+            return copy(gs.at[py * 4 + px], gp.at[m], p_s.at[m], p_r.at[m], rid(py, z, core), px)
+
+        start_all(1, 16, part)
         yield
-        total = gs[q]
-        for m in range(1, 16):
-            ps[m - 1].wait_recv()
-            total = total + gp[m]
+
+        def add(m, total):
+            part(m).wait_recv()
+            return total + gp[m]
+
+        total = lax.fori_loop(1, 16, add, gs[q])
         wide = gz.dtype == BF
         gz[0] = jnp.concatenate([total[:, :128], total[:, 128:]], axis=0).astype(BF) if wide else total
-        zs = []
-        for m in (8, 7, 9, 6, 10, 5, 11, 4, 12, 3, 13, 2, 14, 1, 15):
-            zs.append(send(gz.at[0], gz.at[m], z_s.at[m], z_r.at[m], zpeer(m), x))
+
+        def along_z(n):
+            m = lax.rem(8 + (1 - 2 * lax.rem(n, 2)) * lax.div(n + 1, 2), 16)
+            return copy(gz.at[0], gz.at[m], z_s.at[m], z_r.at[m], zpeer(m), x)
+
+        start_all(0, 15, along_z)
         yield
-        for c in zs:
-            c.wait_recv()
-        total = gz[z].astype(F32)
-        for k in range(1, 16):
-            total = total + gz[lax.rem(z - k + 16, 16)].astype(F32)
+        each(0, 15, lambda n: along_z(n).wait_recv())
+        total = lax.fori_loop(
+            1, 16, lambda k, t: t + gz[lax.rem(z - k + 16, 16)].astype(F32), gz[z].astype(F32)
+        )
         gt[core, q] = jnp.concatenate([total[:8], total[8:]], axis=1) if wide else total
-        ts = []
-        for m in range(1, 16):
-            py, px, pr = peer(m)
-            ts.append(send(gt.at[core, q], gt.at[core, q], t_s.at[m], t_r.at[m], pr, px))
+
+        def whole(m):
+            py, px = rel(m)
+            return copy(gt.at[core, q], gt.at[core, q], t_s.at[m], t_r.at[m], rid(py, z, core), px)
+
+        start_all(1, 16, whole)
         yield
-        for c in ts:
-            c.wait_recv()
+        each(1, 16, lambda m: whole(m).wait_recv())
         c = to_core(gt.at[core], gt.at[core], d_s, d_r)
         yield
         c.wait_recv()
@@ -332,21 +385,38 @@
         tt[:, pl.ds(pl.multiple_of(k * 64, 64), 64), :] = got.reshape(4, 64, 256)
 
     next(reduce2)
-    cc = {}
-    for off in (0, 1, 3, 2):
+
+    def block_copy(off):
         j = lax.rem(y - off + 4, 4)
-        for mx in range(4):
-            if off * 4 + mx:
-                bcopies[off * 4 + mx].wait_recv()
-        cc[off] = to_core(bk.at[j, core], bk.at[j, core], bc_s.at[off], bc_r.at[off])
+        return j, copy(bk.at[j, core], bk.at[j, core], bc_s.at[off], bc_r.at[off], rid(y, z, other), x)
+
+    def own_block(off):
+        j, c = block_copy(off)
+
+        def arrived(mx):
+            @pl.when(off * 4 + mx > 0)
+            def _():
+                back_copy(off * 4 + mx).wait_recv()
+
+        each(0, 4, arrived)
+        c.start()
         slot_terms(j * 2 + core)
+
+    def other_block(off):
+        j, c = block_copy(off)
+        c.wait_recv()
+        slot_terms(j * 2 + other)
+
+    each(0, 4, own_block)
+    pending.append(lambda: each(0, 4, lambda off: block_copy(off)[1].wait_send()))
     next(reduce2)
-    for off in (0, 1, 3, 2):
-        cc[off].wait_recv()
-        slot_terms(lax.rem(y - off + 4, 4) * 2 + other)
+    each(0, 4, other_block)
     yield "bwait"
-    for a in range(4):
-        pb[4 * a:4 * a + 4] = dot(oht[a], tt[a]).astype(BF).reshape(4, 64, 256)
+
+    def row_terms(a):
+        pb[pl.ds(a * 4, 4)] = dot(oht[a], tt[a]).astype(BF).reshape(4, 64, 256)
+
+    each(0, 4, row_terms)
 
     full, parts = pl.ds(0, 64), (pl.ds(0, 32), pl.ds(32, 32))
     fars, nears = {}, {}
@@ -424,7 +494,7 @@
         return pltpu.VMEM(shape, kind)
 
     scratch = [pltpu.VMEM(a.shape, a.dtype) for a in args] + [
-        vmem(BF, 4, 32, 16, 256),
+        vmem(BF, 32, 4, 16, 256),
         vmem(BF, 8, 4, 4, 16, 256),
         vmem(BF, 8, 256, 256),
         vmem(BF, 8, 256, 256),

time: 128 us -> 135 us (1.055)
  Pallas kernels: 124 us -> 131 us
    pallas_call x1, Pallas kernels: 124 us -> 131 us  [local(): pl.pallas_call(kernel, out_shape=(jax.ShapeDtypeStruct((256, 256), BF), j...]
where the time goes in v5:
time: 135 us; the launch traced here: 134 us
  Pallas kernels  131 us (97%)
  local copies, waits for them, and re-layouts  2.98 us (2%)
    pallas_call x1, Pallas kernels, local(): pl.pallas_call(kernel, out_shape=(jax.ShapeDtypeStruct((256, 256), BF), j...  131 us
    unnamed x7, local copies, waits for them, and re-layouts  2.98 us

profile of v5, /device:TPU:1, one launch (start us, length us, event | category | flops | bytes accessed | tf_op | source)
XLA Modules:
  0.0 134.4 jit_solution(12228771290143566464)
XLA Ops:
  0.6 130.7 %shard_map.94 = (bf16[256,256]{1,0:T(8,128)(2,1)}, f32[2,8,8,256]{3,2,1,0:T(8,128)}, f32[256,256]{1,0:T(8,128)}) custom-call(bf16[256,128]{1,0:T(8,128)(2,1)} %refs_0_.1, s32[16,128]{1,0:T(8,128)} %bitcast.5, s32[1,128]{1,0:T(1,128)} %refs_2_.1, bf16[256,2048]{1,0:T(8,128)(2,1)} %refs_3_.1, bf16[128,256]{1,0:T(8,128)(2,1)} %refs_4_.1, ...), custom_call_target="tpu_custom_call" | custom-call | tf_op jit(solution)/shard_map/pallas_call | solution.py:537
  131.4 0.0 copy-start.1
  131.4 0.0 copy-start
  131.4 1.6 %copy.13 = bf16[256,256]{1,0:T(8,128)(2,1)} copy(bf16[256,256]{1,0:T(8,128)(2,1)} %get-tuple-element.12) | data formatting | bytes 262144
  133.0 0.0 copy-done.1
  133.0 0.7 copy.14
  133.7 0.0 copy-done
  133.7 0.7 copy.15
Async XLA Ops:
  131.4 1.6 %copy-start.1 = (f32[2,8,8,256]{3,2,1,0:T(8,128)S(1)}, f32[2,8,8,256]{3,2,1,0:T(8,128)}, u32[]{:S(2)}) copy-start(f32[2,8,8,256]{3,2,1,0:T(8,128)} %get-tuple-element.7) | copy-start | bytes 393220
  131.4 2.3 %copy-start = (f32[256,256]{1,0:T(8,128)S(1)}, f32[256,256]{1,0:T(8,128)}, u32[]{:S(2)}) copy-start(f32[256,256]{1,0:T(8,128)} %get-tuple-element.14) | copy-start | bytes 786436

commit v6 on v3

--- a/solution.py
+++ b/solution.py
@@ -35,7 +35,7 @@
     wtb, wr, wb, wf, stage, g1, oh, oht, pk, mine1, rc1, ab1, rp1, sw, g2,
     mine2, rc2, ab2, rp2, bk, tt, pb, fr, nr, cb,
     in_s, sw_s, sw_r, wx_s, wx_r, z1_s, z1_r, c1_s, c1_r, p1_s, p1_r, sx_s, sx_r, z2_s, z2_r,
-    c2_s, c2_r, p2_s, p2_r, ox_s, ox_r, bp_s, bp_r, bc_s, bc_r, fr_s, fr_r, nr_s, nr_r,
+    c2_s, c2_r, p2_s, p2_r, ox_s, ox_r, bp_s, bp_r, bc_s, bc_r, fr_s, fr_r, nr_r,
     *sums,
 ):
     r = lax.axis_index("rows")
@@ -71,8 +71,13 @@
     def send(src, dst, ssem, rsem, rows, rep):
         c = copy(src, dst, ssem, rsem, rows, rep)
         c.start()
-        pending.append(c.wait_send)
         return c
+
+    def sent(ref, sem):
+        pending.append(copy(ref, ref, sem, sem, rid(y, z, other), x).wait_send)
+
+    def received(ref, sem):
+        copy(ref, ref, sem, sem, rid(y, z, other), x).wait_recv()
 
     def to_core(src, dst, ssem, rsem):
         return send(src, dst, ssem, rsem, rid(y, z, other), x)
@@ -81,14 +86,6 @@
 
     def greet(rows, rep):
         pl.semaphore_signal(barrier, inc=1, device_id={"rows": rows, "rep": rep}, device_id_type=MESH)
-
-    ins = []
-    for n, (a, b) in enumerate(
-        [(feats_h, feats), (idxt_h, idxt), (cnt_h, cnt), (w_h, w), (w1_h, w1), (w2_h, w2), (cot_h, cot)]
-    ):
-        c = pltpu.make_async_copy(a, b, in_s.at[n])
-        c.start()
-        ins.append(c)
 
     alone = x == zb
     swap_r, swap_x = rid(y, za * 4 + x, core), zb
@@ -104,6 +101,14 @@
     def _():
         greet(swap_r, swap_x)
 
+    ins = []
+    for n, (a, b) in enumerate(
+        [(feats_h, feats), (idxt_h, idxt), (cnt_h, cnt), (w_h, w), (w1_h, w1), (w2_h, w2), (cot_h, cot)]
+    ):
+        c = pltpu.make_async_copy(a, b, in_s.at[n])
+        c.start()
+        ins.append(c)
+
     mine = pl.ds(pl.multiple_of(x * 64, 64), 64)
     ins[0].wait()
     ins[1].wait()
@@ -119,7 +124,7 @@
     for sq in range(4):
         alive = [one_hot(cnt[...] > x * 16 + sq * 4 + s4) for s4 in range(4)]
         live = w[:, sq * 512:(sq + 1) * 512] * jnp.concatenate(alive, axis=1)
-        wtb[sq] = dot(order, live, 1, 1).astype(BF).reshape(32, 16, 256)
+        wtb[:, sq] = dot(order, live, 1, 1).astype(BF).reshape(32, 16, 256)
 
     pl.semaphore_wait(barrier, 40 - alone.astype(jnp.int32))
 
@@ -149,15 +154,15 @@
 
     swap_done = swap(stage, g1.at[za * 4 + x], sw_s, sw_r)
 
-    wcopies = []
     me8 = y * 2 + core
-    for m in range(1, 16):
-        py, px, pr = peer(m)
-        for h, hr in ((core, pr), (other, rid(py, z, other))):
-            n = 2 * m + (0 if h is core else 1)
-            wcopies.append(send(wtb.at[:, (py * 4 + px) * 2 + h], wr.at[me8, x], wx_s.at[n], wx_r.at[n], hr, px))
-    wcopies.append(to_core(wtb.at[:, q * 2 + other], wr.at[me8, x], wx_s.at[1], wx_r.at[1]))
-    wr[me8, x] = wtb[:, q * 2 + core]
+    for off in (2, 1, 3, 0):
+        for mx in (2, 1, 3, 0):
+            py, px = lax.rem(y + off, 4), lax.rem(x + mx, 4)
+            for n, h in enumerate((core, other)):
+                if off + mx + n:
+                    send(wtb.at[(py * 4 + px) * 2 + h], wr.at[me8 * 4 + x], wx_s, wx_r, rid(py, z, h), px)
+    sent(wtb.at[pl.ds(0, 31)], wx_s)
+    wr[me8 * 4 + x] = wtb[q * 2 + core]
     yield "prep"
 
     row, col = iota((256, 1), 0), iota((256, 256), 1)
@@ -169,30 +174,26 @@
     def gather_z(g, rows, cut, ssem, rsem, work):
         full, parts = pl.ds(0, rows), (pl.ds(0, cut), pl.ds(cut, rows - cut))
 
-        def move(d, dist):
-            sign = 1 if d == 0 else -1
-            far = dist > 4
-            part = parts[d] if dist == 8 else full
-            slot = zat(-sign * 4) if far else z
-            return copy(g.at[slot, part], g.at[slot, part], ssem.at[d, dist], rsem.at[d, dist],
-                        zpeer(sign * (dist - 4 if far else dist)), x)
-
-        moves = {}
-        for dist in (4, 3, 2, 1):
+        relay = {}
+
+        def move(dist, via):
             for d in range(2):
-                moves[d, dist] = move(d, dist)
-                moves[d, dist].start()
-                pending.append(moves[d, dist].wait_send)
+                sign = 1 if d == 0 else -1
+                if via:
+                    relay[d, via].wait_recv()
+                for there in (6, 8, 5) if dist == 6 else (dist,):
+                    piece = g.at[zat(-sign * via), parts[d] if there == 8 else full]
+                    sem = rsem.at[d * 3 + there // 2 - 1] if there in (2, 4, 6) else rsem.at[6]
+                    relay[d, there] = send(piece, piece, ssem, sem, zpeer(sign * (there - via)), x)
+
+        for dist in (4, 2, 1):
+            move(dist, 0)
         work()
-        for d in range(2):
-            moves[d, 4].wait_recv()
-            for dist in (8, 7, 6, 5):
-                moves[d, dist] = move(d, dist)
-                moves[d, dist].start()
-                pending.append(moves[d, dist].wait_send)
-        for dist in (1, 2, 3, 5, 6, 7, 8):
-            for d in range(2):
-                moves[d, dist].wait_recv()
+        move(3, 2)
+        move(6, 4)
+        move(7, 6)
+        sent(g.at[pl.ds(0, 15)], ssem)
+        received(g.at[pl.ds(0, 9)], rsem.at[6])
 
     gather_z(g1, 80, 48, z1_s, z1_r, lambda: None)
     yield "gz1"
@@ -207,13 +208,12 @@
         pk[a, :, 0:128] = dot(oh[a], g1[4 * a:4 * a + 4, 0:64, :].reshape(256, 128)).astype(BF)
 
     yield "picks1"
-    for c in wcopies:
-        c.wait_recv()
-    yield "wwait"
-
+
+
+    received(wr.at[pl.ds(0, 31)], wx_r)
 
     def weights(k):
-        wb[k] = dot(regroup, wr[k].reshape(256, 256)).astype(BF)
+        wb[k] = dot(regroup, wr[pl.ds(k * 4, 4)].reshape(256, 256)).astype(BF)
         wf[k] = dot(eye, wb[k], 1, 1).astype(BF)
 
     def reduce_planes(width, prepare, own, rc, ab, rp, csem_s, csem_r, psem_s, psem_r):
@@ -227,8 +227,8 @@
         for off in near:
             j = lax.rem(y + off, 4)
             own[j] = partial(j * 2 + other).astype(BF)
-            cs.append(to_core(own.at[j], rc.at[j], csem_s.at[off], csem_r.at[off]))
-        ps = []
+            cs.append(to_core(own.at[j], rc.at[j], csem_s, csem_r.at[off]))
+        sent(own, csem_s)
         for n, off in enumerate(near):
             j = lax.rem(y + off, 4)
             mine_j = partial(j * 2 + core)
@@ -238,10 +238,11 @@
                 m = off * 4 + mx
                 if m:
                     px = lax.rem(x + mx, 4)
-                    ps.append((m, send(ab.at[j, px], rp.at[m], psem_s.at[m], psem_r.at[m], rid(j, z, core), px)))
+                    send(ab.at[j, px], rp.at[m], psem_s, psem_r, rid(j, z, core), px)
+        sent(rp.at[pl.ds(1, 15)], psem_s)
+        received(rp.at[pl.ds(1, 15)], psem_r)
         res = ab[y, x].astype(F32)
-        for m, c in ps[::-1]:
-            c.wait_recv()
+        for m in range(1, 16):
             res = res + rp[m].astype(F32)
         return res.astype(BF)
 
@@ -269,53 +270,52 @@
     z_two = dot(agg2, w2[...])
     dz2 = (cot[mine, :].astype(F32) * silu_slope(z_two)).astype(BF)
     bk[y, core, mine, :] = dot(dz2, w2[...], 1, 1).astype(BF)
-    bcopies = {}
     for off in (2, 1, 3, 0):
         for mx in (2, 1, 3, 0):
             m = off * 4 + mx
             if m:
                 py, px = lax.rem(y + off, 4), lax.rem(x + mx, 4)
-                bcopies[m] = send(bk.at[y, core, mine], bk.at[y, core, mine], bp_s.at[m], bp_r.at[m],
-                                  rid(py, z, core), px)
+                send(bk.at[y, core, mine], bk.at[y, core, mine], bp_s, bp_r.at[off], rid(py, z, core), px)
+    sent(pb.at[pl.ds(0, 15)], bp_s)
     out[mine, :] = (z_two * jax.nn.sigmoid(z_two)).astype(BF)
-    ocopies = []
     for m in range(1, 4):
-        ocopies.append(send(out.at[mine], out.at[mine], ox_s.at[m], ox_r.at[m], r, lax.rem(x + m, 4)))
+        send(out.at[mine], out.at[mine], ox_s, ox_r, r, lax.rem(x + m, 4))
+    sent(out.at[pl.ds(0, 192)], ox_s)
 
     def reduce_all(ga, rc, gs, gp, gz, gt, c_s, c_r, p_s, p_r, z_s, z_r, t_s, t_r, d_s, d_r):
         c = to_core(ga.at[other], rc, c_s, c_r)
+        sent(rc, c_s)
         yield
         c.wait_recv()
         gs[...] = ga[core] + rc[...]
-        ps = []
         for m in range(1, 16):
             py, px, pr = peer(m)
-            ps.append(send(gs.at[py * 4 + px], gp.at[m], p_s.at[m], p_r.at[m], pr, px))
-        yield
+            send(gs.at[py * 4 + px], gp.at[m], p_s, p_r, pr, px)
+        sent(gp.at[pl.ds(1, 15)], p_s)
+        yield
+        received(gp.at[pl.ds(1, 15)], p_r)
         total = gs[q]
         for m in range(1, 16):
-            ps[m - 1].wait_recv()
             total = total + gp[m]
         wide = gz.dtype == BF
         gz[0] = jnp.concatenate([total[:, :128], total[:, 128:]], axis=0).astype(BF) if wide else total
-        zs = []
         for m in (8, 7, 9, 6, 10, 5, 11, 4, 12, 3, 13, 2, 14, 1, 15):
-            zs.append(send(gz.at[0], gz.at[m], z_s.at[m], z_r.at[m], zpeer(m), x))
-        yield
-        for c in zs:
-            c.wait_recv()
+            send(gz.at[0], gz.at[m], z_s, z_r, zpeer(m), x)
+        sent(gz.at[pl.ds(1, 15)], z_s)
+        yield
+        received(gz.at[pl.ds(1, 15)], z_r)
         total = gz[z].astype(F32)
         for k in range(1, 16):
             total = total + gz[lax.rem(z - k + 16, 16)].astype(F32)
         gt[core, q] = jnp.concatenate([total[:8], total[8:]], axis=1) if wide else total
-        ts = []
         for m in range(1, 16):
             py, px, pr = peer(m)
-            ts.append(send(gt.at[core, q], gt.at[core, q], t_s.at[m], t_r.at[m], pr, px))
-        yield
-        for c in ts:
-            c.wait_recv()
+            send(gt.at[core, q], gt.at[core, q], t_s, t_r, pr, px)
+        sent(gt.at[core, pl.ds(0, 15)], t_s)
+        yield
+        received(gt.at[core, pl.ds(0, 15)], t_r)
         c = to_core(gt.at[core], gt.at[core], d_s, d_r)
+        sent(gt.at[core], d_s)
         yield
         c.wait_recv()
         yield
@@ -335,11 +335,10 @@
     cc = {}
     for off in (0, 1, 3, 2):
         j = lax.rem(y - off + 4, 4)
-        for mx in range(4):
-            if off * 4 + mx:
-                bcopies[off * 4 + mx].wait_recv()
-        cc[off] = to_core(bk.at[j, core], bk.at[j, core], bc_s.at[off], bc_r.at[off])
+        received(bk.at[j, core] if off else bk.at[j, core, pl.ds(0, 192)], bp_r.at[off])
+        cc[off] = to_core(bk.at[j, core], bk.at[j, core], bc_s, bc_r.at[off])
         slot_terms(j * 2 + core)
+    sent(bk.at[:, 0], bc_s)
     next(reduce2)
     for off in (0, 1, 3, 2):
         cc[off].wait_recv()
@@ -354,28 +353,29 @@
         for d in range(2):
             sign = 1 if d == 0 else -1
             part = parts[d] if m == 4 else full
-            fars[d, m] = send(pb.at[zat(sign * (4 + m)), part], fr.at[d, m, part], fr_s.at[d, m], fr_r.at[d, m],
+            fars[d, m] = send(pb.at[zat(sign * (4 + m)), part], fr.at[d, m, part], fr_s, fr_r.at[d, 1 if m == 4 else 0],
                               zpeer(sign * m), x)
     for m in (3, 2, 1):
         for d in range(2):
             sign = 1 if d == 0 else -1
-            nears[d, m] = send(pb.at[zat(sign * m)], nr.at[d, m], nr_s.at[d, m], nr_r.at[d, m], zpeer(sign * m), x)
+            nears[d, m] = send(pb.at[zat(sign * m)], nr.at[d, m], fr_s, nr_r.at[d], zpeer(sign * m), x)
     for d in range(2):
         sign = 1 if d == 0 else -1
         acc = pb[zat(sign * 4)].astype(F32)
+        received(fr.at[d, pl.ds(1, 3)], fr_r.at[d, 0])
         for m in (1, 2, 3):
-            fars[d, m].wait_recv()
             acc = acc + fr[d, m].astype(F32)
         fars[d, 4].wait_recv()
         cb[d] = acc.astype(BF)
         lo = 0 if d == 0 else 32
         cb[d, lo:lo + 32, :] = (acc[lo:lo + 32] + fr[d, 4, lo:lo + 32, :].astype(F32)).astype(BF)
-        nears[d, 4] = send(cb.at[d], nr.at[d, 4], nr_s.at[d, 4], nr_r.at[d, 4], zpeer(sign * 4), x)
+        nears[d, 4] = send(cb.at[d], nr.at[d, 4], fr_s, nr_r.at[d], zpeer(sign * 4), x)
     next(reduce2)
     dh = pb[z].astype(F32)
-    for m in (1, 2, 3, 4):
-        for d in range(2):
-            nears[d, m].wait_recv()
+    sent(pb.at[pl.ds(0, 15)], fr_s)
+    for d in range(2):
+        received(nr.at[d, pl.ds(1, 4)], nr_r.at[d])
+        for m in (1, 2, 3, 4):
             dh = dh + nr[d, m].astype(F32)
     yield "rsz"
     dz1 = (dh * silu_slope(z_one)).astype(BF)
@@ -401,8 +401,7 @@
     for b in range(2):
         for k in range(8):
             gr1[:, k, :, b * 128:(b + 1) * 128] = gt1[:, 2 * k + b]
-    for c in ocopies:
-        c.wait_recv()
+    received(out.at[pl.ds(0, 192)], ox_r)
 
 
 def kernel(*refs):
@@ -423,9 +422,10 @@
     def vmem(kind, *shape):
         return pltpu.VMEM(shape, kind)
 
+    one = dma(())
     scratch = [pltpu.VMEM(a.shape, a.dtype) for a in args] + [
-        vmem(BF, 4, 32, 16, 256),
-        vmem(BF, 8, 4, 4, 16, 256),
+        vmem(BF, 32, 4, 16, 256),
+        vmem(BF, 32, 4, 16, 256),
         vmem(BF, 8, 256, 256),
         vmem(BF, 8, 256, 256),
         vmem(BF, 80, 128),
@@ -449,10 +449,10 @@
         vmem(BF, 2, 5, 64, 256),
         vmem(BF, 2, 5, 64, 256),
         vmem(BF, 2, 64, 256),
-        dma((7,)), dma(()), dma(()), dma((32,)), dma((32,)), dma((2, 9)), dma((2, 9)),
-        dma((4,)), dma((4,)), dma((16,)), dma((16,)), dma(()), dma(()), dma((2, 9)), dma((2, 9)),
-        dma((4,)), dma((4,)), dma((16,)), dma((16,)), dma((4,)), dma((4,)), dma((16,)), dma((16,)),
-        dma((4,)), dma((4,)), dma((2, 5)), dma((2, 5)), dma((2, 5)), dma((2, 5)),
+        dma((7,)), one, one, one, one, one, dma((7,)),
+        one, dma((4,)), one, one, one, one, one, dma((7,)),
+        one, dma((4,)), one, one, one, one, one, dma((4,)),
+        one, dma((4,)), one, dma((2, 2)), dma((2,)),
     ]
     for width, first in ((256, (2, 16, 8, 256)), (128, (2, 8, 2, 8, 128))):
         scratch += [
@@ -462,8 +462,7 @@
             vmem(F32, 16, 8, width),
             vmem(BF, 16, 16, 128) if width == 256 else vmem(F32, 16, 8, width),
             vmem(F32, 2, 16, 8, width),
-            dma(()), dma(()), dma((16,)), dma((16,)), dma((16,)), dma((16,)), dma((16,)), dma((16,)), dma(()), dma(()),
-        ]
+        ] + [one] * 10
     out, gr1, gr2 = pl.pallas_call(
         kernel,
         out_shape=(

time: 128 us -> 124 us (0.969)
  Pallas kernels: 124 us -> 121 us
    pallas_call x1, Pallas kernels: 124 us -> 121 us  [local(): pl.pallas_call(kernel, out_shape=(jax.ShapeDtypeStruct((256, 256), BF), j...]
where the time goes in v6:
time: 124 us
  Pallas kernels  121 us (98%)
  local copies, waits for them, and re-layouts  2.98 us (2%)
    pallas_call x1, Pallas kernels, local(): pl.pallas_call(kernel, out_shape=(jax.ShapeDtypeStruct((256, 256), BF), j...  121 us
    unnamed x7, local copies, waits for them, and re-layouts  2.98 us

profile of v6, /device:TPU:1, one launch (start us, length us, event | category | flops | bytes accessed | tf_op | source)
XLA Modules:
  0.0 124.2 jit_solution(4779014076191283875)
XLA Ops:
  0.6 120.6 %shard_map.94 = (bf16[256,256]{1,0:T(8,128)(2,1)}, f32[2,8,8,256]{3,2,1,0:T(8,128)}, f32[256,256]{1,0:T(8,128)}) custom-call(bf16[256,128]{1,0:T(8,128)(2,1)} %refs_0_.1, s32[16,128]{1,0:T(8,128)} %bitcast.5, s32[1,128]{1,0:T(1,128)} %refs_2_.1, bf16[256,2048]{1,0:T(8,128)(2,1)} %refs_3_.1, bf16[128,256]{1,0:T(8,128)(2,1)} %refs_4_.1, ...), custom_call_target="tpu_custom_call" | custom-call | tf_op jit(solution)/shard_map/pallas_call | solution.py:466
  121.2 0.0 copy-start.1
  121.2 0.0 copy-start
  121.2 1.6 %copy.13 = bf16[256,256]{1,0:T(8,128)(2,1)} copy(bf16[256,256]{1,0:T(8,128)(2,1)} %get-tuple-element.12) | data formatting | bytes 262144
  122.8 0.0 copy-done.1
  122.8 0.7 copy.14
  123.5 0.0 copy-done
  123.5 0.7 copy.15
Async XLA Ops:
  121.2 1.6 %copy-start.1 = (f32[2,8,8,256]{3,2,1,0:T(8,128)S(1)}, f32[2,8,8,256]{3,2,1,0:T(8,128)}, u32[]{:S(2)}) copy-start(f32[2,8,8,256]{3,2,1,0:T(8,128)} %get-tuple-element.7) | copy-start | bytes 393220
  121.2 2.3 %copy-start = (f32[256,256]{1,0:T(8,128)S(1)}, f32[256,256]{1,0:T(8,128)}, u32[]{:S(2)}) copy-start(f32[256,256]{1,0:T(8,128)} %get-tuple-element.14) | copy-start | bytes 786436

commit v7 on v6

--- a/solution.py
+++ b/solution.py
@@ -32,8 +32,8 @@
     feats_h, idxt_h, cnt_h, w_h, w1_h, w2_h, cot_h,
     out, gr1, gr2,
     feats, idxt, cnt, w, w1, w2, cot,
-    wtb, wr, wb, wf, stage, g1, oh, oht, pk, mine1, rc1, ab1, rp1, sw, g2,
-    mine2, rc2, ab2, rp2, bk, tt, pb, fr, nr, cb,
+    wtb, wr, wb, wf, stage, g1, oh, oht, pk, own, rc, ab, rp, sw, g2,
+    bk, tt, pb, fr, nr, cb,
     in_s, sw_s, sw_r, wx_s, wx_r, z1_s, z1_r, c1_s, c1_r, p1_s, p1_r, sx_s, sx_r, z2_s, z2_r,
     c2_s, c2_r, p2_s, p2_r, ox_s, ox_r, bp_s, bp_r, bc_s, bc_r, fr_s, fr_r, nr_r,
     *sums,
@@ -160,7 +160,7 @@
             py, px = lax.rem(y + off, 4), lax.rem(x + mx, 4)
             for n, h in enumerate((core, other)):
                 if off + mx + n:
-                    send(wtb.at[(py * 4 + px) * 2 + h], wr.at[me8 * 4 + x], wx_s, wx_r, rid(py, z, h), px)
+                    send(wtb.at[(py * 4 + px) * 2 + h], wr.at[me8 * 4 + x], wx_s, wx_r.at[off], rid(py, z, h), px)
     sent(wtb.at[pl.ds(0, 31)], wx_s)
     wr[me8 * 4 + x] = wtb[q * 2 + core]
     yield "prep"
@@ -171,9 +171,8 @@
     swap_done()
     yield "swap1"
 
-    def gather_z(g, rows, cut, ssem, rsem, work):
+    def gather_z(g, rows, cut, ssem, rsem):
         full, parts = pl.ds(0, rows), (pl.ds(0, cut), pl.ds(cut, rows - cut))
-
         relay = {}
 
         def move(dist, via):
@@ -188,14 +187,18 @@
 
         for dist in (4, 2, 1):
             move(dist, 0)
-        work()
+        yield
         move(3, 2)
         move(6, 4)
+        yield
         move(7, 6)
         sent(g.at[pl.ds(0, 15)], ssem)
+        yield
         received(g.at[pl.ds(0, 9)], rsem.at[6])
-
-    gather_z(g1, 80, 48, z1_s, z1_r, lambda: None)
+        yield
+
+    for _ in gather_z(g1, 80, 48, z1_s, z1_r):
+        pass
     yield "gz1"
 
     ids = g1[:, 64:80, :].reshape(256, 128)
@@ -205,48 +208,60 @@
         rows = dot(ids, one_hot(iota((128, 256), 0) == at))
         oh[:, k * 64:(k + 1) * 64, :] = one_hot(rows == lane).reshape(4, 64, 256)
     for a in range(4):
-        pk[a, :, 0:128] = dot(oh[a], g1[4 * a:4 * a + 4, 0:64, :].reshape(256, 128)).astype(BF)
+        pk[0, a] = dot(oh[a], g1[4 * a:4 * a + 4, 0:64, :].reshape(256, 128)).astype(BF)
 
     yield "picks1"
 
-
-    received(wr.at[pl.ds(0, 31)], wx_r)
 
     def weights(k):
         wb[k] = dot(regroup, wr[pl.ds(k * 4, 4)].reshape(256, 256)).astype(BF)
         wf[k] = dot(eye, wb[k], 1, 1).astype(BF)
 
-    def reduce_planes(width, prepare, own, rc, ab, rp, csem_s, csem_r, psem_s, psem_r):
+    near = (2, 3, 1, 0)
+
+    def reduce_send(t, prepare, csem_s, csem_r, psem_s, psem_r):
         def partial(k):
-            prepare(k)
-            picked = pk[:, pl.ds(pl.multiple_of(k * 64, 64), 64), 0:width].reshape(256, width)
-            return dot(wf[k], picked)
-
-        near = (2, 1, 3, 0)
-        cs = []
-        for off in near:
+            if prepare:
+                prepare(k)
+            return dot(wf[k], pk[t, :, pl.ds(pl.multiple_of(k * 64, 64), 64), :].reshape(256, 128))
+
+        cs, mine_j = [], []
+
+        def first(off):
+            if prepare is weights:
+                received(wr.at[pl.ds(0, 8 if off else 7)], wx_r.at[(4 - off) % 4])
             j = lax.rem(y + off, 4)
-            own[j] = partial(j * 2 + other).astype(BF)
-            cs.append(to_core(own.at[j], rc.at[j], csem_s, csem_r.at[off]))
-        sent(own, csem_s)
-        for n, off in enumerate(near):
+            own[t, j] = partial(j * 2 + other).astype(BF)
+            cs.append(to_core(own.at[t, j], rc.at[t, j], csem_s, csem_r.at[off]))
+            mine_j.append(partial(j * 2 + core))
+
+        def second(n):
+            off = near[n]
             j = lax.rem(y + off, 4)
-            mine_j = partial(j * 2 + core)
             cs[n].wait_recv()
-            ab[j] = (mine_j + rc[j].astype(F32)).astype(BF).reshape(4, 64, width)
-            for mx in near:
-                m = off * 4 + mx
-                if m:
+            ab[t, j] = (mine_j[n] + rc[t, j].astype(F32)).astype(BF).reshape(4, 64, 128)
+            for mx in (2, 1, 3, 0):
+                if off + mx:
                     px = lax.rem(x + mx, 4)
-                    send(ab.at[j, px], rp.at[m], psem_s, psem_r, rid(j, z, core), px)
-        sent(rp.at[pl.ds(1, 15)], psem_s)
-        received(rp.at[pl.ds(1, 15)], psem_r)
-        res = ab[y, x].astype(F32)
+                    send(ab.at[t, j, px], rp.at[t, off * 4 + mx], psem_s, psem_r, rid(j, z, core), px)
+
+        first(near[0])
+        for n in range(1, 4):
+            first(near[n])
+            second(n - 1)
+        second(3)
+        sent(own.at[t], csem_s)
+        sent(rp.at[t, pl.ds(1, 15)], psem_s)
+
+    def reduce_add(t, psem_r):
+        received(rp.at[t, pl.ds(1, 15)], psem_r)
+        res = ab[t, y, x].astype(F32)
         for m in range(1, 16):
-            res = res + rp[m].astype(F32)
+            res = res + rp[t, m].astype(F32)
         return res.astype(BF)
 
-    sw[0] = reduce_planes(128, weights, mine1, rc1, ab1, rp1, c1_s, c1_r, p1_s, p1_r)
+    reduce_send(0, weights, c1_s, c1_r, p1_s, p1_r)
+    sw[0] = reduce_add(0, p1_r)
     yield "red1"
     swap(sw.at[0], sw.at[1], sx_s, sx_r)()
     yield "swap2"
@@ -254,17 +269,23 @@
         ins[n].wait()
     agg1 = sw[1]
     z_one = dot(agg1, w1[...])
-    g2[z] = (z_one * jax.nn.sigmoid(z_one)).astype(BF)
-
-    def turn_picks():
+    hidden = (z_one * jax.nn.sigmoid(z_one)).astype(BF)
+    halves = []
+    for t in range(2):
+        g2[t, z] = hidden[:, t * 128:(t + 1) * 128]
+        halves.append(gather_z(g2.at[t], 64, 32, z2_s.at[t], z2_r.at[t]))
+        next(halves[t])
+    for a in range(4):
+        oht[a] = dot(eye, oh[a], 1, 1).astype(BF)
+    for stage in range(2):
+        for t in range(2):
+            next(halves[t])
+    for t in range(2):
+        next(halves[t])
         for a in range(4):
-            oht[a] = dot(eye, oh[a], 1, 1).astype(BF)
-
-    gather_z(g2, 64, 32, z2_s, z2_r, turn_picks)
-    yield "gz2"
-    for a in range(4):
-        pk[a] = dot(oh[a], g2[4 * a:4 * a + 4].reshape(256, 256)).astype(BF)
-    agg2 = reduce_planes(256, lambda k: None, mine2, rc2, ab2, rp2, c2_s, c2_r, p2_s, p2_r)
+            pk[1 + t, a] = dot(oh[a], g2[t, 4 * a:4 * a + 4].reshape(256, 128)).astype(BF)
+        reduce_send(1 + t, None, c2_s.at[t], c2_r.at[t], p2_s.at[t], p2_r.at[t])
+    agg2 = jnp.concatenate([reduce_add(1 + t, p2_r.at[t]) for t in range(2)], axis=1)
     yield "red2"
 
     z_two = dot(agg2, w2[...])
@@ -282,12 +303,12 @@
         send(out.at[mine], out.at[mine], ox_s, ox_r, r, lax.rem(x + m, 4))
     sent(out.at[pl.ds(0, 192)], ox_s)
 
-    def reduce_all(ga, rc, gs, gp, gz, gt, c_s, c_r, p_s, p_r, z_s, z_r, t_s, t_r, d_s, d_r):
-        c = to_core(ga.at[other], rc, c_s, c_r)
-        sent(rc, c_s)
+    def reduce_all(ga, gc, gs, gp, gz, gt, c_s, c_r, p_s, p_r, z_s, z_r, t_s, t_r, d_s, d_r):
+        c = to_core(ga.at[other], gc, c_s, c_r)
+        sent(gc, c_s)
         yield
         c.wait_recv()
-        gs[...] = ga[core] + rc[...]
+        gs[...] = ga[core] + gc[...]
         for m in range(1, 16):
             py, px, pr = peer(m)
             send(gs.at[py * 4 + px], gp.at[m], p_s, p_r, pr, px)
@@ -432,26 +453,22 @@
         vmem(BF, 16, 80, 128),
         vmem(BF, 4, 512, 256),
         vmem(BF, 4, 256, 512),
-        vmem(BF, 4, 512, 256),
-        vmem(BF, 4, 256, 128),
-        vmem(BF, 4, 256, 128),
-        vmem(BF, 4, 4, 64, 128),
-        vmem(BF, 16, 64, 128),
+        vmem(BF, 3, 4, 512, 128),
+        vmem(BF, 3, 4, 256, 128),
+        vmem(BF, 3, 4, 256, 128),
+        vmem(BF, 3, 4, 4, 64, 128),
+        vmem(BF, 3, 16, 64, 128),
         vmem(BF, 2, 64, 128),
-        vmem(BF, 16, 64, 256),
-        vmem(BF, 4, 256, 256),
-        vmem(BF, 4, 256, 256),
-        vmem(BF, 4, 4, 64, 256),
-        vmem(BF, 16, 64, 256),
+        vmem(BF, 2, 16, 64, 128),
         vmem(BF, 4, 2, 256, 256),
         vmem(BF, 4, 512, 256),
         vmem(BF, 16, 64, 256),
         vmem(BF, 2, 5, 64, 256),
         vmem(BF, 2, 5, 64, 256),
         vmem(BF, 2, 64, 256),
-        dma((7,)), one, one, one, one, one, dma((7,)),
-        one, dma((4,)), one, one, one, one, one, dma((7,)),
-        one, dma((4,)), one, one, one, one, one, dma((4,)),
+        dma((7,)), one, one, one, dma((4,)), one, dma((7,)),
+        one, dma((4,)), one, one, one, one, dma((2,)), dma((2, 7)),
+        dma((2,)), dma((2, 4)), dma((2,)), dma((2,)), one, one, one, dma((4,)),
         one, dma((4,)), one, dma((2, 2)), dma((2,)),
     ]
     for width, first in ((256, (2, 16, 8, 256)), (128, (2, 8, 2, 8, 128))):

time: 124 us -> 123 us (level)
  Pallas kernels: 121 us -> 119 us
where the time goes in v7:
time: 123 us
  Pallas kernels  119 us (97%)
  local copies, waits for them, and re-layouts  2.98 us (2%)
    pallas_call x1, Pallas kernels, local(): pl.pallas_call(kernel, out_shape=(jax.ShapeDtypeStruct((256, 256), BF), j...  119 us
    unnamed x7, local copies, waits for them, and re-layouts  2.98 us

profile of v7, /device:TPU:1, one launch (start us, length us, event | category | flops | bytes accessed | tf_op | source)
XLA Modules:
  0.0 123.1 jit_solution(7390592813117415985)
XLA Ops:
  0.6 119.5 %shard_map.94 = (bf16[256,256]{1,0:T(8,128)(2,1)}, f32[2,8,8,256]{3,2,1,0:T(8,128)}, f32[256,256]{1,0:T(8,128)}) custom-call(bf16[256,128]{1,0:T(8,128)(2,1)} %refs_0_.1, s32[16,128]{1,0:T(8,128)} %bitcast.5, s32[1,128]{1,0:T(1,128)} %refs_2_.1, bf16[256,2048]{1,0:T(8,128)(2,1)} %refs_3_.1, bf16[128,256]{1,0:T(8,128)(2,1)} %refs_4_.1, ...), custom_call_target="tpu_custom_call" | custom-call | tf_op jit(solution)/shard_map/pallas_call | solution.py:483
  120.1 0.0 copy-start.1
  120.1 0.0 copy-start
  120.1 1.6 %copy.13 = bf16[256,256]{1,0:T(8,128)(2,1)} copy(bf16[256,256]{1,0:T(8,128)(2,1)} %get-tuple-element.12) | data formatting | bytes 262144
  121.7 0.0 copy-done.1
  121.8 0.7 copy.14
  122.4 0.0 copy-done
  122.4 0.7 copy.15
Async XLA Ops:
  120.1 1.6 %copy-start.1 = (f32[2,8,8,256]{3,2,1,0:T(8,128)S(1)}, f32[2,8,8,256]{3,2,1,0:T(8,128)}, u32[]{:S(2)}) copy-start(f32[2,8,8,256]{3,2,1,0:T(8,128)} %get-tuple-element.7) | copy-start | bytes 393220
  120.1 2.3 %copy-start = (f32[256,256]{1,0:T(8,128)S(1)}, f32[256,256]{1,0:T(8,128)}, u32[]{:S(2)}) copy-start(f32[256,256]{1,0:T(8,128)} %get-tuple-element.14) | copy-start | bytes 786436

commit v8 on v7

--- a/solution.py
+++ b/solution.py
@@ -35,7 +35,7 @@
     wtb, wr, wb, wf, stage, g1, oh, oht, pk, own, rc, ab, rp, sw, g2,
     bk, tt, pb, fr, nr, cb,
     in_s, sw_s, sw_r, wx_s, wx_r, z1_s, z1_r, c1_s, c1_r, p1_s, p1_r, sx_s, sx_r, z2_s, z2_r,
-    c2_s, c2_r, p2_s, p2_r, ox_s, ox_r, bp_s, bp_r, bc_s, bc_r, fr_s, fr_r, nr_r,
+    c2_s, c2_r, p2_s, p2_r, ox_s, ox_r, bp_s, bp_r, bc_s, bc_r, fr_s, fr_r, nr_r, n3_r,
     *sums,
 ):
     r = lax.axis_index("rows")
@@ -197,8 +197,19 @@
         received(g.at[pl.ds(0, 9)], rsem.at[6])
         yield
 
-    for _ in gather_z(g1, 80, 48, z1_s, z1_r):
-        pass
+    gather1 = gather_z(g1, 80, 48, z1_s, z1_r)
+    for _ in range(3):
+        next(gather1)
+
+    def weights(k):
+        wb[k] = dot(regroup, wr[pl.ds(k * 4, 4)].reshape(256, 256)).astype(BF)
+        wf[k] = dot(eye, wb[k], 1, 1).astype(BF)
+
+    for off in (2, 1, 3, 0):
+        received(wr.at[pl.ds(0, 8 if off else 7)], wx_r.at[off])
+        for h in range(2):
+            weights(lax.rem(y - off + 4, 4) * 2 + h)
+    next(gather1)
     yield "gz1"
 
     ids = g1[:, 64:80, :].reshape(256, 128)
@@ -213,23 +224,15 @@
     yield "picks1"
 
 
-    def weights(k):
-        wb[k] = dot(regroup, wr[pl.ds(k * 4, 4)].reshape(256, 256)).astype(BF)
-        wf[k] = dot(eye, wb[k], 1, 1).astype(BF)
-
     near = (2, 3, 1, 0)
 
-    def reduce_send(t, prepare, csem_s, csem_r, psem_s, psem_r):
+    def reduce_send(t, csem_s, csem_r, psem_s, psem_r):
         def partial(k):
-            if prepare:
-                prepare(k)
             return dot(wf[k], pk[t, :, pl.ds(pl.multiple_of(k * 64, 64), 64), :].reshape(256, 128))
 
         cs, mine_j = [], []
 
         def first(off):
-            if prepare is weights:
-                received(wr.at[pl.ds(0, 8 if off else 7)], wx_r.at[(4 - off) % 4])
             j = lax.rem(y + off, 4)
             own[t, j] = partial(j * 2 + other).astype(BF)
             cs.append(to_core(own.at[t, j], rc.at[t, j], csem_s, csem_r.at[off]))
@@ -260,7 +263,7 @@
             res = res + rp[t, m].astype(F32)
         return res.astype(BF)
 
-    reduce_send(0, weights, c1_s, c1_r, p1_s, p1_r)
+    reduce_send(0, c1_s, c1_r, p1_s, p1_r)
     sw[0] = reduce_add(0, p1_r)
     yield "red1"
     swap(sw.at[0], sw.at[1], sx_s, sx_r)()
@@ -284,20 +287,22 @@
         next(halves[t])
         for a in range(4):
             pk[1 + t, a] = dot(oh[a], g2[t, 4 * a:4 * a + 4].reshape(256, 128)).astype(BF)
-        reduce_send(1 + t, None, c2_s.at[t], c2_r.at[t], p2_s.at[t], p2_r.at[t])
+        reduce_send(1 + t, c2_s.at[t], c2_r.at[t], p2_s.at[t], p2_r.at[t])
     agg2 = jnp.concatenate([reduce_add(1 + t, p2_r.at[t]) for t in range(2)], axis=1)
     yield "red2"
 
     z_two = dot(agg2, w2[...])
     dz2 = (cot[mine, :].astype(F32) * silu_slope(z_two)).astype(BF)
-    bk[y, core, mine, :] = dot(dz2, w2[...], 1, 1).astype(BF)
-    for off in (2, 1, 3, 0):
-        for mx in (2, 1, 3, 0):
-            m = off * 4 + mx
-            if m:
-                py, px = lax.rem(y + off, 4), lax.rem(x + mx, 4)
-                send(bk.at[y, core, mine], bk.at[y, core, mine], bp_s, bp_r.at[off], rid(py, z, core), px)
-    sent(pb.at[pl.ds(0, 15)], bp_s)
+    back = dot(dz2, w2[...], 1, 1).astype(BF)
+    for t in range(2):
+        bk[t, y, core, mine, :] = back[:, t * 128:(t + 1) * 128]
+        piece = bk.at[t, y, core, mine]
+        for off in (2, 1, 3, 0):
+            for mx in (2, 1, 3, 0):
+                if off + mx:
+                    py, px = lax.rem(y + off, 4), lax.rem(x + mx, 4)
+                    send(piece, piece, bp_s.at[t], bp_r.at[t, off], rid(py, z, core), px)
+        sent(pb.at[t, pl.ds(0, 15)], bp_s.at[t])
     out[mine, :] = (z_two * jax.nn.sigmoid(z_two)).astype(BF)
     for m in range(1, 4):
         send(out.at[mine], out.at[mine], ox_s, ox_r, r, lax.rem(x + m, 4))
@@ -347,62 +352,91 @@
     ga2[...] = dot(agg2, dz2, 0, 0).reshape(2, 16, 8, 256)
     next(reduce2)
 
-
-    def slot_terms(k):
-        got = dot(wb[k], bk[lax.div(k, 2), lax.rem(k, 2)]).astype(BF)
-        tt[:, pl.ds(pl.multiple_of(k * 64, 64), 64), :] = got.reshape(4, 64, 256)
+    def slot_terms(t, k):
+        got = dot(wb[k], bk[t, lax.div(k, 2), lax.rem(k, 2)]).astype(BF)
+        tt[t, :, pl.ds(pl.multiple_of(k * 64, 64), 64), :] = got.reshape(4, 64, 128)
 
     next(reduce2)
     cc = {}
-    for off in (0, 1, 3, 2):
-        j = lax.rem(y - off + 4, 4)
-        received(bk.at[j, core] if off else bk.at[j, core, pl.ds(0, 192)], bp_r.at[off])
-        cc[off] = to_core(bk.at[j, core], bk.at[j, core], bc_s, bc_r.at[off])
-        slot_terms(j * 2 + core)
-    sent(bk.at[:, 0], bc_s)
+
+    def own_blocks(t):
+        for off in (0, 1, 3, 2):
+            j = lax.rem(y - off + 4, 4)
+            block = bk.at[t, j, core]
+            received(block if off else bk.at[t, j, core, pl.ds(0, 192)], bp_r.at[t, off])
+            cc[t, off] = to_core(block, block, bc_s.at[t], bc_r.at[t, off])
+            slot_terms(t, j * 2 + core)
+        sent(bk.at[t, :, 0], bc_s.at[t])
+
+    def other_blocks(t):
+        for off in (0, 1, 3, 2):
+            cc[t, off].wait_recv()
+            slot_terms(t, lax.rem(y - off + 4, 4) * 2 + other)
+        for a in range(4):
+            pb[t, 4 * a:4 * a + 4] = dot(oht[a], tt[t, a]).astype(BF).reshape(4, 64, 128)
+
+    full, parts = pl.ds(0, 64), (pl.ds(0, 32), pl.ds(32, 32))
+    ways = ((0, 1), (1, -1))
+    halfway = {}
+
+    def scatter(t):
+        for m in (4, 3, 2, 1):
+            for d, sign in ways:
+                part = parts[d] if m == 4 else full
+                c = send(pb.at[t, zat(sign * (4 + m)), part], fr.at[t, d, m, part], fr_s.at[t],
+                         fr_r.at[t, d, 1 if m == 4 else 0], zpeer(sign * m), x)
+                if m == 4:
+                    halfway[t, d] = c
+        for d, sign in ways:
+            halfway[t, d, 3] = send(pb.at[t, zat(sign * 3)], fr.at[t, d, 0], fr_s.at[t], n3_r.at[t, d], zpeer(sign), x)
+        for d, sign in ways:
+            send(pb.at[t, zat(sign)], nr.at[t, d, 1], fr_s.at[t], nr_r.at[t, d], zpeer(sign), x)
+
+    def pass_near(t):
+        for d, sign in ways:
+            halfway[t, d, 3].wait_recv()
+            cb[t, d, 1] = (pb[t, zat(sign * 2)].astype(F32) + fr[t, d, 0].astype(F32)).astype(BF)
+            send(cb.at[t, d, 1], nr.at[t, d, 2], fr_s.at[t], nr_r.at[t, d], zpeer(sign * 2), x)
+
+    def pass_on(t):
+        for d, sign in ways:
+            acc = pb[t, zat(sign * 4)].astype(F32)
+            received(fr.at[t, d, pl.ds(1, 3)], fr_r.at[t, d, 0])
+            for m in (1, 2, 3):
+                acc = acc + fr[t, d, m].astype(F32)
+            halfway[t, d].wait_recv()
+            lo = 0 if d == 0 else 32
+            cb[t, d, 0] = acc.astype(BF)
+            cb[t, d, 0, lo:lo + 32, :] = (acc[lo:lo + 32] + fr[t, d, 4, lo:lo + 32, :].astype(F32)).astype(BF)
+            send(cb.at[t, d, 0], nr.at[t, d, 3], fr_s.at[t], nr_r.at[t, d], zpeer(sign * 4), x)
+        sent(pb.at[t, pl.ds(0, 15)], fr_s.at[t])
+
+    def collect(t):
+        dh = pb[t, z].astype(F32)
+        for d in range(2):
+            received(nr.at[t, d, pl.ds(1, 3)], nr_r.at[t, d])
+            for m in (1, 2, 3):
+                dh = dh + nr[t, d, m].astype(F32)
+        return dh
+
+    own_blocks(0)
     next(reduce2)
-    for off in (0, 1, 3, 2):
-        cc[off].wait_recv()
-        slot_terms(lax.rem(y - off + 4, 4) * 2 + other)
+    other_blocks(0)
+    scatter(0)
+    own_blocks(1)
+    other_blocks(1)
     yield "bwait"
-    for a in range(4):
-        pb[4 * a:4 * a + 4] = dot(oht[a], tt[a]).astype(BF).reshape(4, 64, 256)
-
-    full, parts = pl.ds(0, 64), (pl.ds(0, 32), pl.ds(32, 32))
-    fars, nears = {}, {}
-    for m in (4, 3, 2, 1):
-        for d in range(2):
-            sign = 1 if d == 0 else -1
-            part = parts[d] if m == 4 else full
-            fars[d, m] = send(pb.at[zat(sign * (4 + m)), part], fr.at[d, m, part], fr_s, fr_r.at[d, 1 if m == 4 else 0],
-                              zpeer(sign * m), x)
-    for m in (3, 2, 1):
-        for d in range(2):
-            sign = 1 if d == 0 else -1
-            nears[d, m] = send(pb.at[zat(sign * m)], nr.at[d, m], fr_s, nr_r.at[d], zpeer(sign * m), x)
-    for d in range(2):
-        sign = 1 if d == 0 else -1
-        acc = pb[zat(sign * 4)].astype(F32)
-        received(fr.at[d, pl.ds(1, 3)], fr_r.at[d, 0])
-        for m in (1, 2, 3):
-            acc = acc + fr[d, m].astype(F32)
-        fars[d, 4].wait_recv()
-        cb[d] = acc.astype(BF)
-        lo = 0 if d == 0 else 32
-        cb[d, lo:lo + 32, :] = (acc[lo:lo + 32] + fr[d, 4, lo:lo + 32, :].astype(F32)).astype(BF)
-        nears[d, 4] = send(cb.at[d], nr.at[d, 4], fr_s, nr_r.at[d], zpeer(sign * 4), x)
+    scatter(1)
+    pass_near(0)
+    slope = silu_slope(z_one)
+    pass_near(1)
+    pass_on(0)
+    pass_on(1)
     next(reduce2)
-    dh = pb[z].astype(F32)
-    sent(pb.at[pl.ds(0, 15)], fr_s)
-    for d in range(2):
-        received(nr.at[d, pl.ds(1, 4)], nr_r.at[d])
-        for m in (1, 2, 3, 4):
-            dh = dh + nr[d, m].astype(F32)
+    for t in range(2):
+        dz1 = (collect(t) * slope[:, t * 128:(t + 1) * 128]).astype(BF)
+        ga1[:, :, t] = dot(agg1, dz1, 0, 0).reshape(2, 8, 8, 128)
     yield "rsz"
-    dz1 = (dh * silu_slope(z_one)).astype(BF)
-    grad1 = dot(agg1, dz1, 0, 0).reshape(2, 8, 8, 256)
-    for b in range(2):
-        ga1[:, :, b] = grad1[:, :, :, b * 128:(b + 1) * 128]
     ga1 = ga1.reshape(2, 16, 8, 128)
     reduce1 = reduce_all(ga1, *sums[half + 1:])
     next(reduce1)
@@ -460,16 +494,16 @@
         vmem(BF, 3, 16, 64, 128),
         vmem(BF, 2, 64, 128),
         vmem(BF, 2, 16, 64, 128),
-        vmem(BF, 4, 2, 256, 256),
-        vmem(BF, 4, 512, 256),
-        vmem(BF, 16, 64, 256),
-        vmem(BF, 2, 5, 64, 256),
-        vmem(BF, 2, 5, 64, 256),
-        vmem(BF, 2, 64, 256),
+        vmem(BF, 2, 4, 2, 256, 128),
+        vmem(BF, 2, 4, 512, 128),
+        vmem(BF, 2, 16, 64, 128),
+        vmem(BF, 2, 2, 5, 64, 128),
+        vmem(BF, 2, 2, 4, 64, 128),
+        vmem(BF, 2, 2, 2, 64, 128),
         dma((7,)), one, one, one, dma((4,)), one, dma((7,)),
         one, dma((4,)), one, one, one, one, dma((2,)), dma((2, 7)),
-        dma((2,)), dma((2, 4)), dma((2,)), dma((2,)), one, one, one, dma((4,)),
-        one, dma((4,)), one, dma((2, 2)), dma((2,)),
+        dma((2,)), dma((2, 4)), dma((2,)), dma((2,)), one, one, dma((2,)), dma((2, 4)),
+        dma((2,)), dma((2, 4)), dma((2,)), dma((2, 2, 2)), dma((2, 2)), dma((2, 2)),
     ]
     for width, first in ((256, (2, 16, 8, 256)), (128, (2, 8, 2, 8, 128))):
         scratch += [

time: 123 us -> 122 us (level)
    pallas_call x1, Pallas kernels: 119 us -> 118 us  [local(): pl.pallas_call(kernel, out_shape=(jax.ShapeDtypeStruct((256, 256), BF), j...]
where the time goes in v8:
time: 122 us; the launch traced here: 121 us
  Pallas kernels  118 us (97%)
  local copies, waits for them, and re-layouts  2.98 us (2%)
    pallas_call x1, Pallas kernels, local(): pl.pallas_call(kernel, out_shape=(jax.ShapeDtypeStruct((256, 256), BF), j...  118 us
    unnamed x7, local copies, waits for them, and re-layouts  2.98 us

profile of v8, /device:TPU:1, one launch (start us, length us, event | category | flops | bytes accessed | tf_op | source)
XLA Modules:
  0.0 121.5 jit_solution(2383196766654314262)
XLA Ops:
  0.6 117.8 %shard_map.94 = (bf16[256,256]{1,0:T(8,128)(2,1)}, f32[2,8,8,256]{3,2,1,0:T(8,128)}, f32[256,256]{1,0:T(8,128)}) custom-call(bf16[256,128]{1,0:T(8,128)(2,1)} %refs_0_.1, s32[16,128]{1,0:T(8,128)} %bitcast.5, s32[1,128]{1,0:T(1,128)} %refs_2_.1, bf16[256,2048]{1,0:T(8,128)(2,1)} %refs_3_.1, bf16[128,256]{1,0:T(8,128)(2,1)} %refs_4_.1, ...), custom_call_target="tpu_custom_call" | custom-call | tf_op jit(solution)/shard_map/pallas_call | solution.py:517
  118.5 0.0 copy-start.1
  118.5 0.0 copy-start
  118.5 1.6 %copy.13 = bf16[256,256]{1,0:T(8,128)(2,1)} copy(bf16[256,256]{1,0:T(8,128)(2,1)} %get-tuple-element.12) | data formatting | bytes 262144
  120.1 0.0 copy-done.1
  120.1 0.7 copy.14
  120.8 0.0 copy-done
  120.8 0.7 copy.15
Async XLA Ops:
  118.5 1.6 %copy-start.1 = (f32[2,8,8,256]{3,2,1,0:T(8,128)S(1)}, f32[2,8,8,256]{3,2,1,0:T(8,128)}, u32[]{:S(2)}) copy-start(f32[2,8,8,256]{3,2,1,0:T(8,128)} %get-tuple-element.7) | copy-start | bytes 393220
  118.5 2.3 %copy-start = (f32[256,256]{1,0:T(8,128)S(1)}, f32[256,256]{1,0:T(8,128)}, u32[]{:S(2)}) copy-start(f32[256,256]{1,0:T(8,128)} %get-tuple-element.14) | copy-start | bytes 786436

commit v9 on v8

--- a/solution.py
+++ b/solution.py
@@ -121,10 +121,13 @@
     plane, rest = row >> 4, row & 15
     source = ((rest >> 2) << 7) + ((plane >> 3) << 5) + ((rest & 3) << 3) + (plane & 7)
     order = one_hot(source == iota((512, 512), 1))
-    for sq in range(4):
+    def regroup_weights(sq):
         alive = [one_hot(cnt[...] > x * 16 + sq * 4 + s4) for s4 in range(4)]
         live = w[:, sq * 512:(sq + 1) * 512] * jnp.concatenate(alive, axis=1)
         wtb[:, sq] = dot(order, live, 1, 1).astype(BF).reshape(32, 16, 256)
+
+    regroup_weights(0)
+    regroup_weights(1)
 
     pl.semaphore_wait(barrier, 40 - alone.astype(jnp.int32))
 
@@ -153,6 +156,8 @@
         return finish
 
     swap_done = swap(stage, g1.at[za * 4 + x], sw_s, sw_r)
+    regroup_weights(2)
+    regroup_weights(3)
 
     me8 = y * 2 + core
     for off in (2, 1, 3, 0):
@@ -333,17 +338,17 @@
         total = gz[z].astype(F32)
         for k in range(1, 16):
             total = total + gz[lax.rem(z - k + 16, 16)].astype(F32)
-        gt[core, q] = jnp.concatenate([total[:8], total[8:]], axis=1) if wide else total
+        gt[q, core] = jnp.concatenate([total[:8], total[8:]], axis=1) if wide else total
+        c = to_core(gt.at[q, core], gt.at[q, core], d_s, d_r)
+        sent(gt.at[q, core], d_s)
+        yield
+        c.wait_recv()
         for m in range(1, 16):
             py, px, pr = peer(m)
-            send(gt.at[core, q], gt.at[core, q], t_s, t_r, pr, px)
-        sent(gt.at[core, pl.ds(0, 15)], t_s)
-        yield
-        received(gt.at[core, pl.ds(0, 15)], t_r)
-        c = to_core(gt.at[core], gt.at[core], d_s, d_r)
-        sent(gt.at[core], d_s)
-        yield
-        c.wait_recv()
+            send(gt.at[q], gt.at[q], t_s, t_r, pr, px)
+        sent(gt.at[pl.ds(0, 15)], t_s)
+        yield
+        received(gt.at[pl.ds(0, 15)], t_r)
         yield
 
     half = len(sums) // 2
@@ -436,15 +441,17 @@
     for t in range(2):
         dz1 = (collect(t) * slope[:, t * 128:(t + 1) * 128]).astype(BF)
         ga1[:, :, t] = dot(agg1, dz1, 0, 0).reshape(2, 8, 8, 128)
+        if t == 0:
+            next(reduce2)
     yield "rsz"
     ga1 = ga1.reshape(2, 16, 8, 128)
     reduce1 = reduce_all(ga1, *sums[half + 1:])
     next(reduce1)
-    next(reduce2)
     yield "arc"
     next(reduce1)
     next(reduce2)
-    gr2[...] = sums[5][...].reshape(256, 256)
+    for n in range(2):
+        gr2[n * 128:(n + 1) * 128, :] = sums[5][:, n].reshape(128, 256)
     yield "arp"
     next(reduce1)
     yield "arz"
@@ -455,7 +462,7 @@
     gt1 = sums[half + 5]
     for b in range(2):
         for k in range(8):
-            gr1[:, k, :, b * 128:(b + 1) * 128] = gt1[:, 2 * k + b]
+            gr1[:, k, :, b * 128:(b + 1) * 128] = gt1[2 * k + b]
     received(out.at[pl.ds(0, 192)], ox_r)
 
 
@@ -512,7 +519,7 @@
             vmem(F32, 16, 8, width),
             vmem(F32, 16, 8, width),
             vmem(BF, 16, 16, 128) if width == 256 else vmem(F32, 16, 8, width),
-            vmem(F32, 2, 16, 8, width),
+            vmem(F32, 16, 2, 8, width),
         ] + [one] * 10
     out, gr1, gr2 = pl.pallas_call(
         kernel,

time: 122 us -> 122 us (level)
  no operation moved by 1% of the time
where the time goes in v9:
time: 122 us
  Pallas kernels  119 us (98%)
  local copies, waits for them, and re-layouts  2.98 us (2%)
    pallas_call x1, Pallas kernels, local(): pl.pallas_call(kernel, out_shape=(jax.ShapeDtypeStruct((256, 256), BF), j...  119 us
    unnamed x7, local copies, waits for them, and re-layouts  2.98 us

profile of v9, /device:TPU:1, one launch (start us, length us, event | category | flops | bytes accessed | tf_op | source)
XLA Modules:
  0.0 122.3 jit_solution(13790603628894678579)
XLA Ops:
  0.6 118.7 %shard_map.94 = (bf16[256,256]{1,0:T(8,128)(2,1)}, f32[2,8,8,256]{3,2,1,0:T(8,128)}, f32[256,256]{1,0:T(8,128)}) custom-call(bf16[256,128]{1,0:T(8,128)(2,1)} %refs_0_.1, s32[16,128]{1,0:T(8,128)} %bitcast.5, s32[1,128]{1,0:T(1,128)} %refs_2_.1, bf16[256,2048]{1,0:T(8,128)(2,1)} %refs_3_.1, bf16[128,256]{1,0:T(8,128)(2,1)} %refs_4_.1, ...), custom_call_target="tpu_custom_call" | custom-call | tf_op jit(solution)/shard_map/pallas_call | solution.py:524
  119.3 0.0 copy-start.1
  119.3 0.0 copy-start
  119.3 1.6 %copy.13 = bf16[256,256]{1,0:T(8,128)(2,1)} copy(bf16[256,256]{1,0:T(8,128)(2,1)} %get-tuple-element.12) | data formatting | bytes 262144
  121.0 0.0 copy-done.1
  121.0 0.7 copy.14
  121.6 0.0 copy-done
  121.6 0.7 copy.15
Async XLA Ops:
  119.3 1.6 %copy-start.1 = (f32[2,8,8,256]{3,2,1,0:T(8,128)S(1)}, f32[2,8,8,256]{3,2,1,0:T(8,128)}, u32[]{:S(2)}) copy-start(f32[2,8,8,256]{3,2,1,0:T(8,128)} %get-tuple-element.7) | copy-start | bytes 393220
  119.3 2.3 %copy-start = (f32[256,256]{1,0:T(8,128)S(1)}, f32[256,256]{1,0:T(8,128)}, u32[]{:S(2)}) copy-start(f32[256,256]{1,0:T(8,128)} %get-tuple-element.14) | copy-start | bytes 786436

commit v10 on v8

--- a/solution.py
+++ b/solution.py
@@ -420,7 +420,6 @@
         return dh
 
     own_blocks(0)
-    next(reduce2)
     other_blocks(0)
     scatter(0)
     own_blocks(1)
@@ -440,15 +439,16 @@
     ga1 = ga1.reshape(2, 16, 8, 128)
     reduce1 = reduce_all(ga1, *sums[half + 1:])
     next(reduce1)
-    next(reduce2)
     yield "arc"
     next(reduce1)
     next(reduce2)
-    gr2[...] = sums[5][...].reshape(256, 256)
     yield "arp"
     next(reduce1)
+    next(reduce2)
     yield "arz"
     next(reduce1)
+    next(reduce2)
+    gr2[...] = sums[5][...].reshape(256, 256)
     yield "art"
     next(reduce1)
     next(reduce1)

time: 122 us -> 120 us (0.984)
  Pallas kernels: 118 us -> 116 us
    pallas_call x1, Pallas kernels: 118 us -> 116 us  [local(): pl.pallas_call(kernel, out_shape=(jax.ShapeDtypeStruct((256, 256), BF), j...]
where the time goes in v10:
time: 120 us
  Pallas kernels  116 us (97%)
  local copies, waits for them, and re-layouts  2.98 us (2%)
    pallas_call x1, Pallas kernels, local(): pl.pallas_call(kernel, out_shape=(jax.ShapeDtypeStruct((256, 256), BF), j...  116 us
    unnamed x7, local copies, waits for them, and re-layouts  2.98 us

profile of v10, /device:TPU:1, one launch (start us, length us, event | category | flops | bytes accessed | tf_op | source)
XLA Modules:
  0.0 119.7 jit_solution(3517708229855401131)
XLA Ops:
  0.6 116.0 %shard_map.94 = (bf16[256,256]{1,0:T(8,128)(2,1)}, f32[2,8,8,256]{3,2,1,0:T(8,128)}, f32[256,256]{1,0:T(8,128)}) custom-call(bf16[256,128]{1,0:T(8,128)(2,1)} %refs_0_.1, s32[16,128]{1,0:T(8,128)} %bitcast.5, s32[1,128]{1,0:T(1,128)} %refs_2_.1, bf16[256,2048]{1,0:T(8,128)(2,1)} %refs_3_.1, bf16[128,256]{1,0:T(8,128)(2,1)} %refs_4_.1, ...), custom_call_target="tpu_custom_call" | custom-call | tf_op jit(solution)/shard_map/pallas_call | solution.py:517
  116.6 0.0 copy-start.1
  116.7 0.0 copy-start
  116.7 1.6 %copy.13 = bf16[256,256]{1,0:T(8,128)(2,1)} copy(bf16[256,256]{1,0:T(8,128)(2,1)} %get-tuple-element.12) | data formatting | bytes 262144
  118.3 0.0 copy-done.1
  118.3 0.7 copy.14
  118.9 0.0 copy-done
  118.9 0.7 copy.15
Async XLA Ops:
  116.6 1.6 %copy-start.1 = (f32[2,8,8,256]{3,2,1,0:T(8,128)S(1)}, f32[2,8,8,256]{3,2,1,0:T(8,128)}, u32[]{:S(2)}) copy-start(f32[2,8,8,256]{3,2,1,0:T(8,128)} %get-tuple-element.7) | copy-start | bytes 393220
  116.7 2.3 %copy-start = (f32[256,256]{1,0:T(8,128)S(1)}, f32[256,256]{1,0:T(8,128)}, u32[]{:S(2)}) copy-start(f32[256,256]{1,0:T(8,128)} %get-tuple-element.14) | copy-start | bytes 786436
